TPU v7x, 32 devices: a whole 2x2x4 slice. The times are simulated.
32 devices in a mesh: hx: 8 (over y, x, core), nb: 4 (over z).
Axes of the slice: x: 2, y: 2, z: 4, core: 2. Of those that a mesh axis runs over, the one named last changes fastest.
Arguments:
- partial_multipoles: bfloat16 [4, 4096, 1464], P('nb', 'hx'), may hold values from -6 to 6
- shared_slots: int32 [4, 4096], P('nb', 'hx'), may hold values from -1 to 1023, as said below
- m2l_sources: int32 [4, 2, 8192], P('nb', None, 'hx'), may hold values from 0 to 1023
- m2l_ops: bfloat16 [2, 1464, 1464], replicated, may hold values from -0.15625 to 0.15625
- positions: float32 [4, 3, 16384], P('nb', None, 'hx'), may hold values from -1 to 1
- forces: float32 [4, 3, 16384], P('nb', None, 'hx'), may hold values from -6 to 6
- leaf_counts: int32 [4, 128], P('nb', 'hx'), may hold values from 32 to 128
- neighbours: int32 [4, 8, 128], P('nb', None, 'hx'), may hold values from 0 to 47
Outputs:
- local_expansion: bfloat16 [4, 8192, 1464], P('nb', 'hx')
- velocity: float32 [4, 3, 16384], P('nb', None, 'hx')
Inputs may be any that keep to these rules, and one draw needn't show every extreme that they name: `shared_slots`: rows j * 64 to (j + 1) * 64 - 1 of each device's 512 rows belong to owner j along hx. Each such block names exactly 16 distinct octants, each at least once; its other rows name one of these or are -1.
All inputs are finite; a program needn't handle non-finite values.
Results may differ from a plain program's by a relative error of at most 0.0048.
Values may be sent and summed in bfloat16 or wider, within the bound.
No kernel may reach another device: no remote copies, remote signals or barrier semaphores. Data moves between devices by JAX's collectives and lax.ppermute only.
A program may use at most 64 MiB of HBM per device.

v0:
```python
import math

import jax
import jax.numpy as jnp
from jax import lax
from jax.sharding import PartitionSpec as P

reg_eps2 = 0.01
inv_eight_pi = 1.0 / (8.0 * math.pi)


def padded(x, sides, width):
    for axis, dim in sides:
        devices, length = (lax.axis_size(axis), x.shape[dim])
        up = [(i, (i + 1) % devices) for i in range(devices - 1)]
        down = [(j, i) for i, j in up]
        last = lax.slice_in_dim(x, length - width, length, axis=dim)
        leading = lax.slice_in_dim(x, 0, width, axis=dim)
        before = lax.ppermute(last, axis, up)
        after = lax.ppermute(leading, axis, down)
        x = jnp.concatenate([before, x, after], axis=dim)
    return x


def leaf_velocity(target_pos, target_live, source_pos, source_frc):
    offset = target_pos[:, None, :] - source_pos[:, :, None]
    dist_sq = jnp.sum(offset * offset, axis=0) + reg_eps2
    inverse_cube = 1.0 / (dist_sq * jnp.sqrt(dist_sq))
    projected = jnp.sum(source_frc[:, :, None] * offset, axis=0)
    summand = (
        source_frc[:, :, None] * (dist_sq + reg_eps2)[None] + projected[None] * offset
    ) * inverse_cube[None]
    return jnp.sum(summand, axis=1) * inv_eight_pi * target_live[None, :]


def leaves_block(own_pos, own_live, leaf_lists, source_table):

    def one_leaf(item):
        leaf_pos, leaf_live, leaf_list = item
        chosen = source_table[:, leaf_list, :].reshape(6, -1)
        return leaf_velocity(leaf_pos, leaf_live, chosen[:3], chosen[3:])

    result = lax.map(one_leaf, (own_pos.transpose(1, 0, 2), own_live, leaf_lists.T))
    return result.transpose(1, 0, 2)


def on_device(
    partial_multipoles,
    shared_slots,
    m2l_sources,
    m2l_ops,
    positions,
    forces,
    leaf_counts,
    neighbours,
):
    hx_count = lax.axis_size("hx")
    shard_rows = partial_multipoles[0]
    coeff_width = shard_rows.shape[1]
    slot_cap = shard_rows.shape[0] // hx_count
    owned = m2l_sources.shape[2]
    slot_rows = shard_rows.reshape(hx_count, slot_cap, coeff_width)
    slot_ids = shared_slots[0].reshape(hx_count, slot_cap)
    octant_range = jnp.arange(owned, dtype=jnp.int32)
    arrived = lax.all_to_all(slot_rows, "hx", split_axis=0, concat_axis=0, tiled=True)
    arrived_ids = lax.all_to_all(slot_ids, "hx", split_axis=0, concat_axis=0, tiled=True)
    one_hot = (arrived_ids.reshape(-1)[None, :] == octant_range[:, None]).astype(jnp.bfloat16)
    summed = jnp.dot(one_hot, arrived.reshape(-1, coeff_width), preferred_element_type=jnp.float32)
    multipoles = summed.astype(jnp.bfloat16)
    total = jnp.zeros((owned, coeff_width), jnp.float32)
    for direction in range(m2l_ops.shape[0]):
        picked = multipoles[m2l_sources[0, direction]]
        total = total + jnp.dot(picked, m2l_ops[direction], preferred_element_type=jnp.float32)
    local_expansion = total.astype(jnp.bfloat16)[None]
    leaf_total = leaf_counts.shape[1]
    per_leaf = positions.shape[2] // leaf_total
    live_mask = (jnp.arange(per_leaf, dtype=jnp.int32)[None, :] < leaf_counts[0][:, None]).astype(
        jnp.float32
    )
    own_pos = positions[0].reshape(3, leaf_total, per_leaf)
    own_frc = forces[0].reshape(3, leaf_total, per_leaf) * live_mask[None]
    packed = jnp.concatenate([own_pos, own_frc], axis=0)[None]
    extended = padded(packed, (("nb", 0),), 1)
    source_table = extended.transpose(1, 0, 2, 3).reshape(6, 3 * leaf_total, per_leaf)
    result = leaves_block(own_pos, live_mask, neighbours[0], source_table)
    velocity = result.reshape(3, leaf_total * per_leaf)[None]
    return (local_expansion, velocity)


def solution(mesh):
    placed = (
        P("nb", "hx", None),
        P("nb", "hx"),
        P("nb", None, "hx"),
        P(),
        P("nb", None, "hx"),
        P("nb", None, "hx"),
        P("nb", "hx"),
        P("nb", None, "hx"),
    )
    return jax.shard_map(
        on_device,
        mesh=mesh,
        in_specs=placed,
        out_specs=(P("nb", "hx", None), P("nb", None, "hx")),
        check_vma=False,
    )
```

profile of v0, /device:TPU:0, one launch (start us, length us, event | category | flops | bytes accessed | tf_op | source)
XLA Modules:
  0.0 118.2 jit_solution(4726879983717051267)
XLA Ops:
  0.6 0.7 fusion.23
  1.4 0.7 broadcast_multiply_fusion
  2.1 0.7 maximum_bitcast_fusion.1
  2.9 1.3 %collective-permute-start.1 = (f32[1,6,16,128]{3,2,1,0:T(8,128)S(1)}, f32[1,6,16,128]{3,2,1,0:T(8,128)S(1)}, u32[]{:S(2)}, u32[]{:S(2)}) collective-permute-start(f32[1,6,16,128]{3,2,1,0:T(8,128)S(1)} %maximum_bitcast_fusion.1), channel_id=1, source_target_pairs={{1,0},{2,1},{3,2},{5,4},{6,5},{7,6},{9,8},{10,9},{11,10},{13,12},{... | collective-permute-start | bytes 147464 | tf_op jit(solution)/shard_map/ppermute | solution.py:20
  4.1 5.6 %collective-permute-start = (f32[1,6,16,128]{3,2,1,0:T(8,128)S(1)}, f32[1,6,16,128]{3,2,1,0:T(8,128)S(1)}, u32[]{:S(2)}, u32[]{:S(2)}) collective-permute-start(f32[1,6,16,128]{3,2,1,0:T(8,128)S(1)} %maximum_bitcast_fusion.1), channel_id=1, source_target_pairs={{0,1},{1,2},{2,3},{4,5},{5,6},{6,7},{8,9},{9,10},{10,11},{12,13},{... | collective-permute-start | bytes 147464 | tf_op jit(solution)/shard_map/ppermute | solution.py:19
  10.2 1.3 %reduce.6 = s32[512]{0:T(512)S(1)} reduce(s32[1,512]{1,0:T(1,128)} %param.11, s32[]{:T(128)} %broadcast.161), dimensions={0}, to_apply=%param.11.reduce_sub_computation.3 | reduce | bytes 4100 | tf_op args[1]
  12.2 4.2 %all-to-all-start = ((s32[8,1,64]{2,1,0:T(1,128)}), s32[8,1,64]{2,1,0:T(1,128)S(1)}, u32[]{:S(2)}, u32[]{:S(2)}) async-start(s32[8,1,64]{2,1,0:T(1,128)} %all_to_all.9), calls=%async_computation | async-start | bytes 8192 | tf_op jit(solution)/shard_map/all_to_all | solution.py:66
  16.3 0.8 compare_select_fusion.2
  17.1 2.6 %copy.30 = bf16[1,512,1464]{2,1,0:T(8,128)(2,1)} copy(bf16[1,512,1464]{1,2,0:T(8,128)(2,1)} %param.10) | data formatting | bytes 2998272 | tf_op args[0]
  19.8 1.1 all-to-all-done
  20.9 3.6 %all-to-all-start.1 = ((bf16[8,64,1464]{2,1,0:T(8,128)(2,1)}), bf16[8,64,1464]{2,1,0:T(8,128)(2,1)S(1)}, u32[]{:S(2)}, u32[]{:S(2)}) async-start(bf16[8,64,1464]{2,1,0:T(8,128)(2,1)} %bitcast.8), calls=%async_computation.1 | async-start | bytes 3145728 | tf_op jit(solution)/shard_map/all_to_all | solution.py:65
  25.2 57.8 %while.12 = (s32[]{:T(128)}, f32[16,3,128]{2,1,0:T(4,128)S(1)}, s32[16,8]{1,0:T(8,128)S(1)}, f32[6,48,128]{2,0,1:T(8,128)S(1)}, f32[16,3,128]{2,0,1:T(8,128)}, /*index=5*/f32[16,128]{1,0:T(8,128)S(1)}, s32[]{:T(128)}) while((s32[]{:T(128)}, f32[16,3,128]{2,1,0:T(4,128)S(1)}, s32[16,8]{1,0:T(8,128)S(1)}, f32[6,48,128]{2,0,1:T(8,128)S(1)}, ...), condition=%wide.region_4.5_spmd, body=%wide.region_0.4_spmd.sunk | while | flops 4588698 | bytes 4362469 | solution.py:43
  25.9 0.7 constant_dynamic-slice_fusion.4
  26.6 1.0 fusion.33
  27.8 1.0 fusion.34
  29.5 0.7 constant_dynamic-slice_fusion.4
  30.2 1.0 fusion.33
  31.4 1.0 fusion.34
  33.1 0.7 constant_dynamic-slice_fusion.4
  33.8 1.0 fusion.33
  35.1 1.0 fusion.34
  36.7 0.7 constant_dynamic-slice_fusion.4
  37.4 1.0 fusion.33
  38.7 1.0 fusion.34
  40.3 0.7 constant_dynamic-slice_fusion.4
  41.0 1.0 fusion.33
  42.3 1.0 fusion.34
  43.9 0.7 constant_dynamic-slice_fusion.4
  44.7 1.0 fusion.33
  45.9 1.0 fusion.34
  47.5 0.7 constant_dynamic-slice_fusion.4
  48.3 1.0 fusion.33
  49.5 1.0 fusion.34
  51.2 0.7 constant_dynamic-slice_fusion.4
  51.9 1.0 fusion.33
  53.1 1.0 fusion.34
  54.8 0.7 constant_dynamic-slice_fusion.4
  55.5 1.0 fusion.33
  56.7 1.0 fusion.34
  59.1 1.0 fusion.33
  60.4 1.0 fusion.34
  62.0 0.7 constant_dynamic-slice_fusion.4
  62.7 1.0 fusion.33
  64.0 1.0 fusion.34
  65.6 0.7 constant_dynamic-slice_fusion.4
  66.3 1.0 fusion.33
  67.6 1.0 fusion.34
  69.2 0.7 constant_dynamic-slice_fusion.4
  70.0 1.0 fusion.33
  71.2 1.0 fusion.34
  73.6 1.0 fusion.33
  74.8 1.0 fusion.34
  76.5 0.7 constant_dynamic-slice_fusion.4
  77.2 1.0 fusion.33
  78.4 1.0 fusion.34
  80.1 0.7 constant_dynamic-slice_fusion.4
  80.8 1.0 fusion.33
  82.0 1.0 fusion.34
  83.7 3.4 %convolution_convert_fusion = bf16[1024,1464]{0,1:T(8,128)(2,1)} fusion(bf16[512,1464]{1,0:T(8,128)(2,1)S(1)} %bitcast.75, s32[512]{0:T(512)S(1)} %eq.15), kind=kOutput, calls=%fused_computation.35 | convolution fusion | flops 1537138688 | bytes 4499456 | tf_op jit(solution)/shard_map/dot_general | solution.py:68
  87.1 3.1 %copy.31 = bf16[1024,1464]{1,0:T(8,128)(2,1)S(1)} copy(bf16[1024,1464]{0,1:T(8,128)(2,1)} %convolution_convert_fusion) | data formatting | bytes 5996544 | tf_op jit(solution)/shard_map/convert_element_type | solution.py:69
  90.3 5.6 %gather_fusion.2 = bf16[1024,1464]{1,0:T(8,128)(2,1)} fusion(bf16[1024,1464]{1,0:T(8,128)(2,1)S(1)} %copy.31, s32[1024]{0:T(1024)S(1)} %broadcast_clamp_fusion), kind=kCustom, calls=%fused_computation.2 | custom fusion | bytes 6000640 | tf_op jit(solution)/shard_map/gather | solution.py:72
  95.9 5.6 %gather_fusion.1 = bf16[1024,1464]{1,0:T(8,128)(2,1)} fusion(bf16[1024,1464]{1,0:T(8,128)(2,1)S(1)} %copy.31, s32[1024]{0:T(1024)S(1)} %broadcast_clamp_fusion.1), kind=kCustom, calls=%fused_computation.1 | custom fusion | bytes 6000640 | tf_op jit(solution)/shard_map/gather | solution.py:72
  101.4 8.2 %fusion.11 = f32[1024,1464]{0,1:T(8,128)S(1)} fusion(bf16[1024,1464]{1,0:T(8,128)(2,1)} %gather_fusion.2, bf16[2,1464,1464]{2,1,0:T(8,128)(2,1)} %param.13), kind=kOutput, calls=%fused_computation.29 | convolution fusion | flops 4389470208 | bytes 13639680 | tf_op jit(solution)/shard_map/dot_general | solution.py:73
  109.7 8.5 %fusion.19 = bf16[1,1024,1464]{1,2,0:T(8,128)(2,1)} fusion(f32[1024,1464]{0,1:T(8,128)S(1)} %fusion.11, bf16[1024,1464]{1,0:T(8,128)(2,1)S(1)} %copy-done, bf16[2,1464,1464]{2,1,0:T(8,128)(2,1)} %param.13), kind=kOutput, calls=%fused_computation.36 | convolution fusion | flops 4392468480 | bytes 16490496 | tf_op jit(solution)/shard_map/dot_general | solution.py:73
  (149 shorter events, 17.0 us)
Async XLA Ops:
  0.6 19.1 %copy-start.1 = (s32[1,8,16]{2,1,0:T(8,128)S(1)}, s32[1,8,16]{2,1,0:T(8,128)}, u32[]{:S(2)}) copy-start(s32[1,8,16]{2,1,0:T(8,128)} %param.17) | copy-start | bytes 1540
  2.9 22.3 %collective-permute-start.1 = (f32[1,6,16,128]{3,2,1,0:T(8,128)S(1)}, f32[1,6,16,128]{3,2,1,0:T(8,128)S(1)}, u32[]{:S(2)}, u32[]{:S(2)}) collective-permute-start(f32[1,6,16,128]{3,2,1,0:T(8,128)S(1)} %maximum_bitcast_fusion.1), channel_id=1, source_target_pairs={{1,0},{2,1},{3,2},{5,4},{6,5},{7,6},{9,8},{10,9},{11,10},{13,12},{... | collective-permute-start | bytes 147464 | tf_op jit(solution)/shard_map/ppermute | solution.py:20
  4.1 21.0 %collective-permute-start = (f32[1,6,16,128]{3,2,1,0:T(8,128)S(1)}, f32[1,6,16,128]{3,2,1,0:T(8,128)S(1)}, u32[]{:S(2)}, u32[]{:S(2)}) collective-permute-start(f32[1,6,16,128]{3,2,1,0:T(8,128)S(1)} %maximum_bitcast_fusion.1), channel_id=1, source_target_pairs={{0,1},{1,2},{2,3},{4,5},{5,6},{6,7},{8,9},{9,10},{10,11},{12,13},{... | collective-permute-start | bytes 147464 | tf_op jit(solution)/shard_map/ppermute | solution.py:19
  12.2 8.7 %all-to-all-start = ((s32[8,1,64]{2,1,0:T(1,128)}), s32[8,1,64]{2,1,0:T(1,128)S(1)}, u32[]{:S(2)}, u32[]{:S(2)}) async-start(s32[8,1,64]{2,1,0:T(1,128)} %all_to_all.9), calls=%async_computation | async-start | bytes 8192 | tf_op jit(solution)/shard_map/all_to_all | solution.py:66
  20.9 62.8 %all-to-all-start.1 = ((bf16[8,64,1464]{2,1,0:T(8,128)(2,1)}), bf16[8,64,1464]{2,1,0:T(8,128)(2,1)S(1)}, u32[]{:S(2)}, u32[]{:S(2)}) async-start(bf16[8,64,1464]{2,1,0:T(8,128)(2,1)} %bitcast.8), calls=%async_computation.1 | async-start | bytes 3145728 | tf_op jit(solution)/shard_map/all_to_all | solution.py:65
  101.4 8.2 %copy-start = (bf16[1024,1464]{1,0:T(8,128)(2,1)S(1)}, bf16[1024,1464]{1,0:T(8,128)(2,1)}, u32[]{:S(2)}) copy-start(bf16[1024,1464]{1,0:T(8,128)(2,1)} %gather_fusion.1) | copy-start | bytes 8994820
where the time goes:
time: 120 us; the launch traced here: 118 us
  other arithmetic  40.9 us (34%)
  local copies, waits for them, and re-layouts  39.5 us (33%)
  matrix products  20.2 us (17%)
  starting transfers between devices  14.6 us (12%)
    dot_general x2, matrix products, on_device(): jnp.dot(picked, m2l_ops[direction], preferred_element_type=jnp.float32)  16.7 us
    reduce_sum x16, other arithmetic, leaf_velocity(): projected = jnp.sum(source_frc[:, :, None] * offset, axis=0)  16.4 us
    reduce_sum x16, other arithmetic, leaf_velocity(): return jnp.sum(summand, axis=1) * inv_eight_pi * target_live[None, :]  15.8 us
    dynamic_slice x32, local copies, waits for them, and re-layouts, leaves_block(): lax.map(one_leaf, (own_pos.transpose(1, 0, 2), own_live, leaf_lists.T))  11.6 us
    gather x2, local copies, waits for them, and re-layouts, on_device(): picked = multipoles[m2l_sources[0, direction]]  11.2 us
    gather x16, local copies, waits for them, and re-layouts, one_leaf(): chosen = source_table[:, leaf_list, :].reshape(6, -1)  8.88 us
    ppermute x1, starting transfers between devices, padded(): before = lax.ppermute(last, axis, up)  5.56 us
    all_to_all x1, starting transfers between devices, on_device(): lax.all_to_all(slot_ids, 'hx', split_axis=0, concat_axis=0, tiled=True)  4.16 us
  transfers between devices with their start and end apart: 4, of which 1 were waited for; matrix products, arithmetic and copies ran while one was open for 53% of the time, Pallas kernels for 0%

commit v1 on v0

v1 whole, which is shorter than its diff:
```python
import functools
import math

import jax
import jax.numpy as jnp
from jax import lax
from jax.experimental import pallas as pl
from jax.experimental.pallas import tpu as pltpu
from jax.sharding import PartitionSpec as P

reg_eps2 = 0.01
inv_eight_pi = 1.0 / (8.0 * math.pi)
id_base = 32
lanes = 128
bf16 = jnp.bfloat16
f32 = jnp.float32


def split(value, count):
    pieces = []
    for _ in range(count):
        piece = value.astype(bf16).astype(f32)
        pieces.append(piece)
        value = value - piece
    return pieces


def presum_kernel(
    cap, uniq, counts_hbm, slots_hbm, rows_hbm, pos_hbm, frc_hbm, neighbours_hbm,
    sums_ref, packed_ref, counts_out, neighbours_out,
    counts_ref, slots_ref, rows_ref, pos_ref, frc_ref, arrival,
):
    pairs = (
        (slots_hbm, slots_ref),
        (counts_hbm, counts_ref),
        (pos_hbm, pos_ref),
        (frc_hbm, frc_ref),
        (counts_hbm, counts_out),
        (neighbours_hbm, neighbours_out),
        (rows_hbm, rows_ref),
    )
    copies = [pltpu.make_async_copy(a, b, arrival.at[i]) for i, (a, b) in enumerate(pairs)]
    for copy in copies:
        copy.start()
    for copy in copies[:-1]:
        copy.wait()

    leaves, per_leaf = pos_ref.shape[1:]
    leaf_at = lax.broadcasted_iota(jnp.int32, (leaves, per_leaf), 0)
    point_at = lax.broadcasted_iota(jnp.int32, (leaves, per_leaf), 1)
    count = jnp.zeros((leaves, per_leaf), jnp.int32)
    for leaf in range(leaves):
        count = jnp.where(leaf_at == leaf, counts_ref[0, leaf], count)
    live = (point_at < count).astype(f32)
    for axis in range(3):
        packed_ref[axis] = pos_ref[axis]
        packed_ref[3 + axis] = frc_ref[axis] * live

    coeffs, row_count = rows_ref.shape
    slot_count = sums_ref.shape[0]
    targets, firsts = [], []
    sub_at = lax.broadcasted_iota(jnp.int32, (lanes, lanes), 0)
    lane_at = lax.broadcasted_iota(jnp.int32, (lanes, lanes), 1)
    same_block = (sub_at // cap) == (lane_at // cap)
    for start in range(0, row_count, lanes):
        by_lane = jnp.broadcast_to(slots_ref[:, start : start + lanes], (lanes, lanes))
        by_sub = by_lane.T
        equal = same_block & (by_lane == by_sub)
        seen = jnp.where(equal & (lane_at < sub_at), 1, 0)
        first = (jnp.max(seen, axis=1, keepdims=True) == 0) & (by_sub >= 0)
        below = jnp.where(first & same_block & (by_sub < by_lane), 1, 0)
        rank = jnp.sum(below, axis=0, keepdims=True)
        lane_row = lax.broadcasted_iota(jnp.int32, (1, lanes), 1) + start
        block = lane_row // cap
        valid = slots_ref[:, start : start + lanes] >= 0
        targets.append(jnp.where(valid, block * uniq + rank, -1))
    target = jnp.concatenate(targets, axis=1)
    slot_at = lax.broadcasted_iota(jnp.int32, (slot_count, row_count), 0)
    hit = slot_at == target
    octant = jnp.max(jnp.where(hit, slots_ref[...], -1), axis=1, keepdims=True)
    one_hot = jnp.where(hit, 1.0, 0.0).astype(bf16)
    copies[-1].wait()
    sums = lax.dot_general(
        one_hot, rows_ref[...], (((1,), (1,)), ((), ())), preferred_element_type=f32
    )
    sums_ref[:, :coeffs] = sums.astype(bf16)
    high = octant // id_base
    low = octant - high * id_base
    extra_at = lax.broadcasted_iota(jnp.int32, (slot_count, sums_ref.shape[1] - coeffs), 1)
    extra = jnp.where(extra_at == 0, high, jnp.where(extra_at == 1, low, 0))
    sums_ref[:, coeffs:] = extra.astype(f32).astype(bf16)


def near_kernel(
    slab_axis, neighbours_ref, counts_ref, own_ref, even_ref, odd_ref, out_ref,
    wide_ref, source_ref, target_wide_ref, target_ref,
):
    _, leaves, per_leaf = own_ref.shape
    group = 8
    wide = 3 * group
    deep = 4 * group
    nbr_count = neighbours_ref.shape[1]
    even = lax.rem(lax.axis_index(slab_axis), 2) == 0

    def stored(ref, leaf_start, height, row, value):
        ref[pl.ds(leaf_start * height + row, leaves, stride=height), :] = value

    for part in range(3):
        if part == 0:
            comp = [jnp.where(even, odd_ref[c], even_ref[c]) for c in range(6)]
        elif part == 1:
            comp = [own_ref[c] for c in range(6)]
        else:
            comp = [jnp.where(even, even_ref[c], odd_ref[c]) for c in range(6)]
        cut = [split(c, 2) for c in comp]
        kept = [high + low for high, low in cut]
        norm = kept[0] * kept[0] + kept[1] * kept[1] + kept[2] * kept[2]
        size = split(norm + reg_eps2, 3)
        along = split(-(kept[0] * kept[3] + kept[1] * kept[4] + kept[2] * kept[5]), 3)
        for piece in range(2):
            rows = [cut[c][piece] for c in range(6)] + [size[piece], along[piece]]
            for row, value in enumerate(rows):
                stored(wide_ref, part * leaves, wide, piece * group + row, value)
        stored(wide_ref, part * leaves, wide, 2 * group, size[2])
        stored(wide_ref, part * leaves, wide, 2 * group + 1, along[2])
        if part == 1:
            norm = split(norm, 3)
            zero, one = jnp.zeros_like(norm[0]), jnp.ones_like(norm[0])
            for piece in range(2):
                fill = [one, one] if piece == 0 else [zero, zero]
                rows = [-2.0 * cut[c][piece] for c in range(3)] + [cut[c][piece] for c in range(3)] + fill
                for row, value in enumerate(rows):
                    stored(target_wide_ref, 0, 2 * wide, piece * 2 * group + row, value)
                    stored(target_wide_ref, 0, 2 * wide, piece * 2 * group + group + row, value)
            for row, value in enumerate([one, one] + norm + [zero] * (2 * group - 5)):
                stored(target_wide_ref, 0, 2 * wide, 4 * group + row, value)

    row_at = lax.broadcasted_iota(jnp.int32, (group, per_leaf), 0)
    left = (row_at < 3) | (row_at == 6)
    left_ones = (row_at >= 2) & (row_at < 5)
    for leaf in range(3 * leaves):
        high, low, rest = [wide_ref[pl.ds(leaf * wide + i * group, group), :] for i in range(3)]
        for half in range(2):
            if half == 0:
                tail = jnp.where(row_at == 0, rest, jnp.where(left_ones, 1.0, 0.0))
                pieces = [jnp.where(left, high, 0.0), jnp.where(left, low, 0.0), tail]
            else:
                tail = jnp.where(row_at == 1, rest, 0.0)
                pieces = [jnp.where(left, 0.0, high), jnp.where(left, 0.0, low), tail]
            pieces.append(jnp.zeros((group, per_leaf), f32))
            block = jnp.concatenate(pieces, axis=0).astype(bf16)
            source_ref[pl.ds(leaf * deep, deep), pl.ds(half * per_leaf, per_leaf)] = block
    for leaf in range(leaves):
        block = target_wide_ref[pl.ds(leaf * 2 * wide, 2 * wide), :]
        target_ref[pl.ds(leaf * per_leaf, per_leaf), :] = block.T.astype(bf16)

    def one_leaf(leaf, carry):
        target = target_ref[pl.ds(pl.multiple_of(leaf * per_leaf, per_leaf), per_leaf), :]
        total = jnp.zeros((per_leaf, deep), f32)
        for n in range(nbr_count):
            source = neighbours_ref[0, n, leaf]
            block = source_ref[pl.ds(pl.multiple_of(source * deep, deep), deep), :]
            features = jnp.concatenate([block[: 2 * group], block], axis=0)
            both = jnp.dot(target, features, preferred_element_type=f32)
            dist_sq, projected = both[:, :per_leaf], both[:, per_leaf:]
            inverse = lax.rsqrt(dist_sq)
            cube = inverse * inverse * inverse
            along_f = inverse + reg_eps2 * cube
            along_d = projected * cube
            pair = jnp.concatenate([along_d.astype(bf16), along_f.astype(bf16)], axis=1)
            total = total + lax.dot_general(
                pair, block, (((1,), (1,)), ((), ())), preferred_element_type=f32
            )
        turned = total.T
        live = lax.broadcasted_iota(jnp.int32, (1, per_leaf), 1) < counts_ref[0, leaf]
        factor = jnp.where(live, inv_eight_pi, 0.0)
        weight = turned[18:19]
        for axis in range(3):
            own = own_ref[axis, pl.ds(leaf, 1), :]
            along_f = turned[3 + axis : 4 + axis] + turned[11 + axis : 12 + axis]
            along_y = turned[axis : axis + 1] + turned[8 + axis : 9 + axis]
            out_ref[axis, pl.ds(leaf, 1), :] = (along_f + (own * weight - along_y)) * factor
        return carry

    lax.fori_loop(0, leaves, one_leaf, 0, unroll=8)


def far_kernel(sources_ref, rows_ref, ops_hbm, out_hbm, ops_ref, pick_ref, moved_ref, out_ref, ops_sem, out_sem):
    coeffs = ops_hbm.shape[1]
    directions = ops_hbm.shape[0]
    slot_count = rows_ref.shape[0]
    tile = moved_ref.shape[1]
    spans = [(start, min(tile, coeffs - start)) for start in range(0, coeffs, tile)]

    loads = []
    for i, (start, size) in enumerate(spans):
        at = pl.ds(start, size)
        loads.append(pltpu.make_async_copy(ops_hbm.at[:, :, at], ops_ref.at[:, :, at], ops_sem.at[i]))
        loads[-1].start()

    octant = rows_ref[:, coeffs : coeffs + 2].astype(f32).astype(jnp.int32)
    octant = octant[:, :1] * id_base + octant[:, 1:]
    for t in range(directions):
        hit = octant == sources_ref[0, t : t + 1, :]
        pick_ref[t * slot_count : (t + 1) * slot_count, :] = jnp.where(hit, 1.0, 0.0).astype(bf16)
    rows = rows_ref[:, :coeffs]
    stores = []
    for i, (start, size) in enumerate(spans):
        loads[i].wait()
        for t in range(directions):
            moved = jnp.dot(rows, ops_ref[t, :, start : start + size], preferred_element_type=f32)
            moved_ref[t * slot_count : (t + 1) * slot_count, :size] = moved.astype(bf16)
        total = lax.dot_general(
            moved_ref[:, :size], pick_ref[...], (((0,), (0,)), ((), ())), preferred_element_type=f32
        )
        out_ref[start : start + size, :] = total.astype(bf16)
        at = pl.ds(start, size)
        stores.append(pltpu.make_async_copy(out_ref.at[at, :], out_hbm.at[at, :], out_sem.at[i]))
        stores[-1].start()
    for store in stores:
        store.wait()


def vmem():
    return pl.BlockSpec(memory_space=pltpu.VMEM)


def in_hbm(array):
    return pltpu.with_memory_space_constraint(array, pltpu.HBM)


def smem():
    return pl.BlockSpec(memory_space=pltpu.SMEM)


def call_near(neighbours, leaf_counts, packed, even, odd):
    _, leaves, per_leaf = packed.shape
    table = 3 * leaves
    return pl.pallas_call(
        functools.partial(near_kernel, "nb"),
        out_shape=jax.ShapeDtypeStruct((3, leaves, per_leaf), f32),
        in_specs=[smem(), smem()] + [vmem()] * 3,
        out_specs=vmem(),
        scratch_shapes=[
            pltpu.VMEM((table * 24, per_leaf), f32),
            pltpu.VMEM((table * 32, 2 * per_leaf), bf16),
            pltpu.VMEM((leaves * 48, per_leaf), f32),
            pltpu.VMEM((leaves * per_leaf, 48), bf16),
        ],
        compiler_params=pltpu.CompilerParams(vmem_limit_bytes=24 * 2**20),
        cost_estimate=pl.CostEstimate(flops=8 * 10**9, bytes_accessed=10**6, transcendentals=2 * 10**6),
        name="near",
    )(neighbours, leaf_counts, packed, even, odd)


def on_device(
    partial_multipoles,
    shared_slots,
    m2l_sources,
    m2l_ops,
    positions,
    forces,
    leaf_counts,
    neighbours,
):
    hx_count, nb_count = lax.axis_size("hx"), lax.axis_size("nb")
    row_count, coeffs = partial_multipoles.shape[1:]
    cap = row_count // hx_count
    uniq = cap // 4
    slot_count = hx_count * uniq
    width = -(-(coeffs + 2) // lanes) * lanes
    leaves = leaf_counts.shape[1]
    per_leaf = positions.shape[2] // leaves
    owned = m2l_sources.shape[2]
    directions = m2l_ops.shape[0]

    sums, packed, counts, sources = pl.pallas_call(
        functools.partial(presum_kernel, cap, uniq),
        out_shape=(
            pltpu.VMEM((slot_count, width), bf16),
            pltpu.VMEM((6, leaves, per_leaf), f32),
            pltpu.VMEM(leaf_counts.shape, jnp.int32),
            pltpu.VMEM(neighbours.shape, jnp.int32),
        ),
        in_specs=[pl.BlockSpec(memory_space=pltpu.HBM)] * 6,
        out_specs=(vmem(), vmem(), vmem(), vmem()),
        scratch_shapes=[
            pltpu.SMEM(leaf_counts.shape, jnp.int32),
            pltpu.VMEM(shared_slots.shape, jnp.int32),
            pltpu.VMEM((coeffs, row_count), bf16),
            pltpu.VMEM((3, leaves, per_leaf), f32),
            pltpu.VMEM((3, leaves, per_leaf), f32),
            pltpu.SemaphoreType.DMA((7,)),
        ],
        compiler_params=pltpu.CompilerParams(vmem_limit_bytes=16 * 2**20),
        name="presum",
    )(
        *map(
            in_hbm,
            (
                leaf_counts,
                shared_slots,
                partial_multipoles[0].T,
                positions[0].reshape(3, leaves, per_leaf),
                forces[0].reshape(3, leaves, per_leaf),
                neighbours,
            ),
        )
    )

    even_pairs = [(i, i + 1) for i in range(0, nb_count - 1, 2)]
    odd_pairs = [(i, i + 1) for i in range(1, nb_count - 1, 2)]
    odd = lax.ppermute(packed, "nb", odd_pairs + [(j, i) for i, j in odd_pairs])
    even = lax.ppermute(packed, "nb", even_pairs + [(j, i) for i, j in even_pairs])
    arrived = lax.all_to_all(
        sums.reshape(hx_count, uniq, width), "hx", split_axis=0, concat_axis=0, tiled=True
    ).reshape(slot_count, width)

    velocity = call_near(sources, counts, packed, even, odd)

    tile = 2 * lanes
    steps = -(-coeffs // tile)
    local = pl.pallas_call(
        far_kernel,
        out_shape=jax.ShapeDtypeStruct((coeffs, owned), bf16),
        in_specs=[vmem(), vmem(), pl.BlockSpec(memory_space=pltpu.HBM)],
        out_specs=pl.BlockSpec(memory_space=pltpu.HBM),
        scratch_shapes=[
            pltpu.VMEM(m2l_ops.shape, bf16),
            pltpu.VMEM((directions * slot_count, owned), bf16),
            pltpu.VMEM((directions * slot_count, tile), bf16),
            pltpu.VMEM((coeffs, owned), bf16),
            pltpu.SemaphoreType.DMA((steps,)),
            pltpu.SemaphoreType.DMA((steps,)),
        ],
        compiler_params=pltpu.CompilerParams(vmem_limit_bytes=32 * 2**20),
        name="far",
    )(m2l_sources, arrived, in_hbm(m2l_ops))

    return local.T[None], velocity.reshape(1, 3, leaves * per_leaf)


def solution(mesh):
    placed = (
        P("nb", "hx", None),
        P("nb", "hx"),
        P("nb", None, "hx"),
        P(),
        P("nb", None, "hx"),
        P("nb", None, "hx"),
        P("nb", "hx"),
        P("nb", None, "hx"),
    )
    return jax.shard_map(
        on_device,
        mesh=mesh,
        in_specs=placed,
        out_specs=(P("nb", "hx", None), P("nb", None, "hx")),
        check_vma=False,
    )
```

time: 120 us -> 28.8 us (0.24); the launches traced: 118 us -> 28.6 us
  other arithmetic: 40.9 us -> 0 us
  local copies, waits for them, and re-layouts: 39.5 us -> 0.01 us
  matrix products: 20.2 us -> 0 us
  Pallas kernels: 0 us -> 16.2 us
  starting transfers between devices: 14.6 us -> 10.3 us
    reduce_sum x32 -> x0, other arithmetic: 32.2 us -> none  [the longest x16 16.4 us: leaf_velocity(): projected = jnp.sum(source_frc[:, :, None] * offset, axis=0)]
    dot_general x3 -> x0, matrix products: 20.2 us -> none  [the longest x2 16.7 us: on_device(): jnp.dot(picked, m2l_ops[direction], preferred_element_type=jnp.float32)]
    gather x18 -> x0, local copies, waits for them, and re-layouts: 20 us -> none  [the longest x2 11.2 us: on_device(): picked = multipoles[m2l_sources[0, direction]]]
    pallas_call x0 -> x3, Pallas kernels: none -> 16.2 us  [the longest x1 6.91 us: call_near(): pl.pallas_call(functools.partial(near_kernel, 'nb'), out_shape=jax.ShapeD...]
    dynamic_slice x32 -> x0, local copies, waits for them, and re-layouts: 11.6 us -> none  [leaves_block(): lax.map(one_leaf, (own_pos.transpose(1, 0, 2), own_live, leaf_lists.T))]
    all_to_all x2 -> x1, starting transfers between devices: 7.74 us -> 3.73 us  [on_device(): lax.all_to_all(sums.reshape(hx_count, uniq, width), 'hx', split_axis=0, c...]
    add x16 -> x0, other arithmetic: 3.16 us -> none  [leaf_velocity(): dist_sq + reg_eps2]
    convert_element_type x1 -> x0, local copies, waits for them, and re-layouts: 3.15 us -> none  [on_device(): multipoles = summed.astype(jnp.bfloat16)]
  transfers between devices with their start and end apart: 4 -> 3, of which waited for: 1 -> 1; matrix products, arithmetic and copies ran while one was open for 53% -> 0% of each run, Pallas kernels for 0% -> 24%
where the time goes in v1:
time: 28.8 us; the launch traced here: 28.6 us
  Pallas kernels  16.2 us (56%)
  starting transfers between devices  10.3 us (36%)
  waiting for transfers between devices  1.4 us (5%)
  between operations  0.67 us (2%)
    pallas_call x1, Pallas kernels, call_near(): pl.pallas_call(functools.partial(near_kernel, 'nb'), out_shape=jax.ShapeD...  6.91 us
    pallas_call x1, Pallas kernels, on_device(): pl.pallas_call(far_kernel, out_shape=jax.ShapeDtypeStruct((coeffs, owned)...  6.39 us
    ppermute x1, starting transfers between devices, on_device(): lax.ppermute(packed, 'nb', even_pairs + [(j, i) for i, j in even_pairs])  5.9 us
    all_to_all x1, starting transfers between devices, on_device(): lax.all_to_all(sums.reshape(hx_count, uniq, width), 'hx', split_axis=0, c...  3.73 us
    pallas_call x1, Pallas kernels, on_device(): pl.pallas_call(functools.partial(presum_kernel, cap, uniq), out_shape=(pl...  2.9 us
    all_to_all x1, waiting for transfers between devices, on_device(): lax.all_to_all(sums.reshape(hx_count, uniq, width), 'hx', split_axis=0, c...  1.4 us
    ppermute x1, starting transfers between devices, on_device(): odd = lax.ppermute(packed, 'nb', odd_pairs + [(j, i) for i, j in odd_pairs])  0.66 us
  transfers between devices with their start and end apart: 3, of which 1 were waited for; matrix products, arithmetic and copies ran while one was open for 0% of the time, Pallas kernels for 24%

profile of v1, /device:TPU:0, one launch (start us, length us, event | category | flops | bytes accessed | tf_op | source)
XLA Modules:
  0.0 28.6 jit_solution(16894147346087475054)
XLA Ops:
  0.6 2.9 %presum.1 = (bf16[128,1536]{1,0:T(8,128)(2,1)}, f32[6,16,128]{2,1,0:T(8,128)S(1)}, s32[1,16]{1,0:T(1,128)S(1)}, s32[1,8,16]{2,1,0:T(8,128)S(1)}) custom-call(s32[1,16]{1,0:T(1,128)} %counts_hbm.1, s32[1,512]{1,0:T(1,128)} %slots_hbm.1, bf16[1464,512]{1,0:T(8,128)(2,1)} %bitcast.13, f32[3,16,128]{2,1,0:T(8,128)} %bitcast.14, f32[3,16,128]{2,1,0:T(8,128)} %bitcast.15, ...), custom_call_target="tpu_custom_call" | custom-call | tf_op jit(solution)/shard_map/presum/pallas_call | solution.py:277
  3.5 0.7 %collective-permute-start.1 = (f32[6,16,128]{2,1,0:T(8,128)S(1)}, f32[6,16,128]{2,1,0:T(8,128)S(1)}, u32[]{:S(2)}, u32[]{:S(2)}) collective-permute-start(f32[6,16,128]{2,1,0:T(8,128)S(1)} %get-tuple-element.9.own_ref), channel_id=1, source_target_pairs={{1,2},{2,1},{5,6},{6,5},{9,10},{10,9},{13,14},{14,13},{17,18},{18,... | collective-permute-start | bytes 147464 | tf_op jit(solution)/shard_map/ppermute | solution.py:313
  4.2 5.9 %collective-permute-start = (f32[6,16,128]{2,1,0:T(8,128)S(1)}, f32[6,16,128]{2,1,0:T(8,128)S(1)}, u32[]{:S(2)}, u32[]{:S(2)}) collective-permute-start(f32[6,16,128]{2,1,0:T(8,128)S(1)} %get-tuple-element.9.own_ref), channel_id=1, source_target_pairs={{0,1},{2,3},{1,0},{3,2},{4,5},{6,7},{5,4},{7,6},{8,9},{10,11},{9,8... | collective-permute-start | bytes 147464 | tf_op jit(solution)/shard_map/ppermute | solution.py:314
  10.1 3.7 %all-to-all-start = ((bf16[8,16,1536]{2,1,0:T(8,128)(2,1)}), bf16[8,16,1536]{2,1,0:T(8,128)(2,1)S(1)}, u32[]{:S(2)}, u32[]{:S(2)}) async-start(bf16[8,16,1536]{2,1,0:T(8,128)(2,1)} %bitcast.4), calls=%async_computation | async-start | bytes 786432 | tf_op jit(solution)/shard_map/all_to_all | solution.py:315
  13.8 0.0 collective-permute-done.1.odd_ref
  13.9 0.0 collective-permute-done.even_ref
  13.9 0.0 copy-start
  13.9 6.9 %near.1 = f32[3,16,128]{2,1,0:T(8,128)} custom-call(s32[1,8,16]{2,1,0:T(8,128)S(1)} %get-tuple-element.7.neighbours_ref, s32[1,16]{1,0:T(1,128)S(1)} %get-tuple-element.8.counts_ref, f32[6,16,128]{2,1,0:T(8,128)S(1)} %get-tuple-element.9.own_ref, f32[6,16,128]{2,1,0:T(8,128)S(1)} %collective-permute-done.even_ref, ...), custom_call_target="tpu_custom_call" | custom-call | flops 8000000000 | bytes 1000000 | tf_op jit(solution)/shard_map/near/pallas_call | solution.py:239
  20.8 1.4 %all-to-all-done = bf16[8,16,1536]{2,1,0:T(8,128)(2,1)S(1)} async-done(((bf16[8,16,1536]{2,1,0:T(8,128)(2,1)}), bf16[8,16,1536]{2,1,0:T(8,128)(2,1)S(1)}, u32[]{:S(2)}, u32[]{:S(2)}) %all-to-all-start) | async-done | bytes 393248 | tf_op jit(solution)/shard_map/all_to_all | solution.py:315
  22.2 0.0 copy-done
  22.2 6.4 %far.1 = bf16[1464,1024]{1,0:T(8,128)(2,1)} custom-call(s32[1,2,1024]{2,1,0:T(2,128)S(1)} %copy-done, bf16[128,1536]{1,0:T(8,128)(2,1)S(1)} %bitcast.11, bf16[2,1464,1464]{2,1,0:T(8,128)(2,1)} %ops_hbm.1), custom_call_target="tpu_custom_call" | custom-call | tf_op jit(solution)/shard_map/far/pallas_call | solution.py:323
Async XLA Ops:
  3.5 10.3 %collective-permute-start.1 = (f32[6,16,128]{2,1,0:T(8,128)S(1)}, f32[6,16,128]{2,1,0:T(8,128)S(1)}, u32[]{:S(2)}, u32[]{:S(2)}) collective-permute-start(f32[6,16,128]{2,1,0:T(8,128)S(1)} %get-tuple-element.9.own_ref), channel_id=1, source_target_pairs={{1,2},{2,1},{5,6},{6,5},{9,10},{10,9},{13,14},{14,13},{17,18},{18,... | collective-permute-start | bytes 147464 | tf_op jit(solution)/shard_map/ppermute | solution.py:313
  4.2 9.6 %collective-permute-start = (f32[6,16,128]{2,1,0:T(8,128)S(1)}, f32[6,16,128]{2,1,0:T(8,128)S(1)}, u32[]{:S(2)}, u32[]{:S(2)}) collective-permute-start(f32[6,16,128]{2,1,0:T(8,128)S(1)} %get-tuple-element.9.own_ref), channel_id=1, source_target_pairs={{0,1},{2,3},{1,0},{3,2},{4,5},{6,7},{5,4},{7,6},{8,9},{10,11},{9,8... | collective-permute-start | bytes 147464 | tf_op jit(solution)/shard_map/ppermute | solution.py:314
  10.1 12.1 %all-to-all-start = ((bf16[8,16,1536]{2,1,0:T(8,128)(2,1)}), bf16[8,16,1536]{2,1,0:T(8,128)(2,1)S(1)}, u32[]{:S(2)}, u32[]{:S(2)}) async-start(bf16[8,16,1536]{2,1,0:T(8,128)(2,1)} %bitcast.4), calls=%async_computation | async-start | bytes 786432 | tf_op jit(solution)/shard_map/all_to_all | solution.py:315
  13.9 8.3 %copy-start = (s32[1,2,1024]{2,1,0:T(2,128)S(1)}, s32[1,2,1024]{2,1,0:T(2,128)}, u32[]{:S(2)}) copy-start(s32[1,2,1024]{2,1,0:T(2,128)} %sources_ref.1) | copy-start | bytes 24580

commit v2 on v1

v2 whole, which is shorter than its diff:
```python
import functools
import math

import jax
import jax.numpy as jnp
from jax import lax
from jax.experimental import pallas as pl
from jax.experimental.pallas import tpu as pltpu
from jax.sharding import PartitionSpec as P

reg_eps2 = 0.01
inv_eight_pi = 1.0 / (8.0 * math.pi)
id_base = 32
lanes = 128
bf16 = jnp.bfloat16
f32 = jnp.float32


def split(value, count):
    pieces = []
    for _ in range(count):
        piece = value.astype(bf16).astype(f32)
        pieces.append(piece)
        value = value - piece
    return pieces


def presum_kernel(
    cap, uniq, tile, counts_hbm, slots_hbm, rows_hbm, pos_hbm, frc_hbm, neighbours_hbm,
    sums_hbm, packed_ref, counts_out, neighbours_out,
    counts_ref, slots_ref, rows_ref, pos_ref, frc_ref, sums_ref, arrival, rows_sem, sums_sem,
):
    coeffs, row_count = rows_ref.shape
    slot_count, width = sums_ref.shape
    spans = [(start, min(tile, coeffs - start)) for start in range(0, coeffs, tile)]
    pairs = (
        (slots_hbm, slots_ref),
        (counts_hbm, counts_ref),
        (pos_hbm, pos_ref),
        (frc_hbm, frc_ref),
        (counts_hbm, counts_out),
        (neighbours_hbm, neighbours_out),
    )
    copies = [pltpu.make_async_copy(a, b, arrival.at[i]) for i, (a, b) in enumerate(pairs)]
    loads = []
    for i, (start, size) in enumerate(spans):
        at = pl.ds(start, size)
        loads.append(pltpu.make_async_copy(rows_hbm.at[at, :], rows_ref.at[at, :], rows_sem.at[i]))
    for copy in copies[:1] + loads + copies[1:]:
        copy.start()
    copies[0].wait()

    targets = []
    sub_at = lax.broadcasted_iota(jnp.int32, (lanes, lanes), 0)
    lane_at = lax.broadcasted_iota(jnp.int32, (lanes, lanes), 1)
    same_block = (sub_at // cap) == (lane_at // cap)
    for start in range(0, row_count, lanes):
        by_lane = jnp.broadcast_to(slots_ref[:, start : start + lanes], (lanes, lanes))
        by_sub = by_lane.T
        equal = same_block & (by_lane == by_sub)
        seen = jnp.where(equal & (lane_at < sub_at), 1, 0)
        first = (jnp.max(seen, axis=1, keepdims=True) == 0) & (by_sub >= 0)
        below = jnp.where(first & same_block & (by_sub < by_lane), 1, 0)
        rank = jnp.sum(below, axis=0, keepdims=True)
        lane_row = lax.broadcasted_iota(jnp.int32, (1, lanes), 1) + start
        block = lane_row // cap
        valid = slots_ref[:, start : start + lanes] >= 0
        targets.append(jnp.where(valid, block * uniq + rank, -1))
    target = jnp.concatenate(targets, axis=1)
    slot_at = lax.broadcasted_iota(jnp.int32, (slot_count, row_count), 0)
    hit = slot_at == target
    octant = jnp.max(jnp.where(hit, slots_ref[...], -1), axis=1, keepdims=True)
    one_hot = jnp.where(hit, 1.0, 0.0).astype(bf16)
    high = octant // id_base
    low = octant - high * id_base
    extra_at = lax.broadcasted_iota(jnp.int32, (slot_count, width - coeffs), 1)
    extra = jnp.where(extra_at == 0, high, jnp.where(extra_at == 1, low, 0))
    sums_ref[:, coeffs:] = extra.astype(f32).astype(bf16)
    stores = []
    for i, (start, size) in enumerate(spans):
        loads[i].wait()
        sums = lax.dot_general(
            one_hot,
            rows_ref[start : start + size, :],
            (((1,), (1,)), ((), ())),
            preferred_element_type=f32,
        )
        sums_ref[:, start : start + size] = sums.astype(bf16)
        at = pl.ds(start, min(tile, width - start))
        stores.append(pltpu.make_async_copy(sums_ref.at[:, at], sums_hbm.at[:, at], sums_sem.at[i]))
        stores[-1].start()
    for copy in copies[1:]:
        copy.wait()
    leaves, per_leaf = pos_ref.shape[1:]
    leaf_at = lax.broadcasted_iota(jnp.int32, (leaves, per_leaf), 0)
    point_at = lax.broadcasted_iota(jnp.int32, (leaves, per_leaf), 1)
    count = jnp.zeros((leaves, per_leaf), jnp.int32)
    for leaf in range(leaves):
        count = jnp.where(leaf_at == leaf, counts_ref[0, leaf], count)
    live = (point_at < count).astype(f32)
    for axis in range(3):
        packed_ref[axis] = pos_ref[axis]
        packed_ref[3 + axis] = frc_ref[axis] * live
    for store in stores:
        store.wait()


def near_field(
    slab_axis, lists, neighbours_ref, counts_ref, own_ref, even_ref, odd_ref, out_ref,
    point_ref, moment_ref, source_ref, weight_ref, target_wide_ref, target_ref, sums_ref,
):
    _, leaves, per_leaf = own_ref.shape
    group = 16
    pieces = 3
    nbr_count = neighbours_ref.shape[1]
    even = lax.rem(lax.axis_index(slab_axis), 2) == 0
    one = jnp.ones((leaves, per_leaf), f32)

    def stored(ref, leaf_start, height, rows):
        for row, value in enumerate(rows):
            ref[pl.ds(leaf_start * height + row, leaves, stride=height), :] = value

    def dot3(left, right):
        return left[0] * right[0] + left[1] * right[1] + left[2] * right[2]

    own_cut = None
    for part in range(3):
        if part == 0:
            comp = [jnp.where(even, odd_ref[c], even_ref[c]) for c in range(6)]
        elif part == 1:
            comp = [own_ref[c] for c in range(6)]
        else:
            comp = [jnp.where(even, even_ref[c], odd_ref[c]) for c in range(6)]
        cut = [split(c, 2) for c in comp[:3]]
        place = [high + low for high, low in cut]
        force = comp[3:]
        norm = dot3(place, place)
        along = dot3(force, place)
        size = split(norm + reg_eps2, 3)
        stored(point_ref, part * leaves, group, [c[0] for c in cut] + [c[1] for c in cut] + size)
        moments = force + [force[i] * place[j] for i in range(3) for j in range(3)]
        moments += [force[i] * (norm + 2.0 * reg_eps2) + along * place[i] for i in range(3)]
        stored(moment_ref, part * leaves, group, moments)
        if part == 1:
            own_cut, own_norm, own_place = cut, norm, place
    high = [-2.0 * c[0] for c in own_cut]
    low = [-2.0 * c[1] for c in own_cut]
    zero = jnp.zeros_like(one)
    rows = high + high + [one] * 3 + split(own_norm, 3) + [zero] * 4 + low + low + [zero] * 10
    stored(target_wide_ref, 0, 2 * group, rows)

    row_at = lax.broadcasted_iota(jnp.int32, (group, per_leaf), 0)
    for leaf in range(3 * leaves):
        at = pl.ds(leaf * group, group)
        point = jnp.where(row_at < 9, point_ref[at, :], jnp.where(row_at < 12, 1.0, 0.0))
        source_ref[at, :] = point.astype(bf16)
        moment = jnp.where(row_at < 15, moment_ref[at, :], 0.0)
        for i, piece in enumerate(split(moment, pieces)):
            weight_ref[pl.ds((leaf * pieces + i) * group, group), :] = piece.astype(bf16)
    for leaf in range(leaves):
        block = target_wide_ref[pl.ds(leaf * 2 * group, 2 * group), :]
        target_ref[pl.ds(leaf * per_leaf, per_leaf), :] = block.T.astype(bf16)

    for copy in lists:
        copy.wait()

    def one_leaf(leaf, carry):
        target = target_ref[pl.ds(pl.multiple_of(leaf * per_leaf, per_leaf), per_leaf), :]
        total = jnp.zeros((per_leaf, pieces * group), f32)
        for n in range(0, nbr_count, 2):
            near = [neighbours_ref[0, n + k, leaf] for k in range(2)]
            points = [source_ref[pl.ds(pl.multiple_of(s * group, group), group), :] for s in near]
            deep = pieces * group
            weights = [weight_ref[pl.ds(pl.multiple_of(s * deep, group), deep), :] for s in near]
            points = jnp.concatenate(points, axis=1)
            dist_sq = jnp.dot(
                target, jnp.concatenate([points, points], axis=0), preferred_element_type=f32
            )
            inverse = lax.rsqrt(dist_sq)
            cube = (inverse * inverse * inverse).astype(bf16)
            total = total + lax.dot_general(
                cube,
                jnp.concatenate(weights, axis=1),
                (((1,), (1,)), ((), ())),
                preferred_element_type=f32,
            )
        turned = total.T
        sums = turned[:group] + turned[group : 2 * group] + turned[2 * group :]
        sums_ref[pl.ds(leaf, group, stride=leaves), :] = sums
        return carry

    lax.fori_loop(0, leaves, one_leaf, 0, unroll=8)

    got = [sums_ref[pl.ds(row * leaves, leaves), :] for row in range(15)]
    first, mixed, rest = got[:3], [got[3 + 3 * i : 6 + 3 * i] for i in range(3)], got[12:]
    leaf_at = lax.broadcasted_iota(jnp.int32, (leaves, per_leaf), 0)
    point_at = lax.broadcasted_iota(jnp.int32, (leaves, per_leaf), 1)
    count = jnp.zeros((leaves, per_leaf), jnp.int32)
    for leaf in range(leaves):
        count = jnp.where(leaf_at == leaf, counts_ref[0, leaf], count)
    factor = jnp.where(point_at < count, inv_eight_pi, 0.0)
    shift = dot3(own_place, first) - (mixed[0][0] + mixed[1][1] + mixed[2][2])
    for i in range(3):
        turned = dot3(own_place, [2.0 * mixed[i][j] + mixed[j][i] for j in range(3)])
        out_ref[i] = (own_norm * first[i] + own_place[i] * shift - turned + rest[i]) * factor


def far_field(sources_ref, rows_ref, ops_ref, out_ref, out_hbm, pick_ref, moved_ref, out_sem, ready):
    directions, coeffs, _ = ops_ref.shape
    slot_count = rows_ref.shape[0]
    tile = moved_ref.shape[1]
    octant = rows_ref[:, coeffs : coeffs + 2].astype(f32).astype(jnp.int32)
    octant = octant[:, :1] * id_base + octant[:, 1:]
    for t in range(directions):
        hit = octant == sources_ref[0, t : t + 1, :]
        pick_ref[t * slot_count : (t + 1) * slot_count, :] = jnp.where(hit, 1.0, 0.0).astype(bf16)
    rows = rows_ref[:, :coeffs]
    stores = []
    for i, start in enumerate(range(0, coeffs, tile)):
        ready(i)
        size = min(tile, coeffs - start)
        for t in range(directions):
            moved = jnp.dot(rows, ops_ref[t, :, start : start + size], preferred_element_type=f32)
            moved_ref[t * slot_count : (t + 1) * slot_count, :size] = moved.astype(bf16)
        for low in range(0, size, 2 * lanes):
            rest = min(2 * lanes, size - low)
            total = lax.dot_general(
                moved_ref[:, low : low + rest],
                pick_ref[...],
                (((0,), (0,)), ((), ())),
                preferred_element_type=f32,
            )
            at = pl.ds(start + low, rest)
            out_ref[at, :] = total.astype(bf16)
            sem = out_sem.at[len(stores)]
            stores.append(pltpu.make_async_copy(out_ref.at[at, :], out_hbm.at[at, :], sem))
            stores[-1].start()
    return stores


def fields_kernel(
    slab_axis, neighbours_vmem, counts_vmem, own_ref, odd_ref, even_ref, picks_hbm, rows_ref, ops_hbm,
    velocity_hbm, local_hbm,
    neighbours_ref, counts_ref, velocity_ref,
    point_ref, moment_ref, source_ref, weight_ref, target_wide_ref, target_ref, sums_ref,
    picks_ref, ops_ref, pick_ref, moved_ref, local_ref, ops_sem, out_sem,
):
    coeffs, tile = ops_hbm.shape[1], moved_ref.shape[1]
    steps = -(-coeffs // tile)
    lists = (
        pltpu.make_async_copy(neighbours_vmem, neighbours_ref, ops_sem.at[steps + 1]),
        pltpu.make_async_copy(counts_vmem, counts_ref, ops_sem.at[steps + 2]),
    )
    for copy in lists:
        copy.start()
    picks_load = pltpu.make_async_copy(picks_hbm, picks_ref, ops_sem.at[steps])
    picks_load.start()
    loads = []
    for i, start in enumerate(range(0, coeffs, tile)):
        at = pl.ds(start, min(tile, coeffs - start))
        loads.append(pltpu.make_async_copy(ops_hbm.at[:, :, at], ops_ref.at[:, :, at], ops_sem.at[i]))
        loads[-1].start()
    near_field(
        slab_axis, lists, neighbours_ref, counts_ref, own_ref, even_ref, odd_ref, velocity_ref,
        point_ref, moment_ref, source_ref, weight_ref, target_wide_ref, target_ref, sums_ref,
    )
    velocity_store = pltpu.make_async_copy(velocity_ref, velocity_hbm, ops_sem.at[steps + 3])
    velocity_store.start()
    picks_load.wait()
    stores = far_field(
        picks_ref, rows_ref, ops_ref, local_ref, local_hbm, pick_ref, moved_ref, out_sem,
        lambda i: loads[i].wait(),
    )
    for store in stores + [velocity_store]:
        store.wait()


def vmem():
    return pl.BlockSpec(memory_space=pltpu.VMEM)


def in_hbm(array):
    return pltpu.with_memory_space_constraint(array, pltpu.HBM)


def hbm():
    return pl.BlockSpec(memory_space=pltpu.HBM)


def call_fields(neighbours, leaf_counts, packed, even, odd, m2l_sources, arrived, m2l_ops):
    _, leaves, per_leaf = packed.shape
    directions, coeffs, _ = m2l_ops.shape
    owned = m2l_sources.shape[2]
    slot_count = arrived.shape[0]
    tile = 4 * lanes
    steps = -(-coeffs // tile)
    table = 3 * leaves
    picks = directions * slot_count
    return pl.pallas_call(
        functools.partial(fields_kernel, "nb"),
        out_shape=(
            jax.ShapeDtypeStruct((3, leaves, per_leaf), f32),
            jax.ShapeDtypeStruct((coeffs, owned), bf16),
        ),
        in_specs=[vmem(), vmem(), vmem(), vmem(), vmem(), hbm(), vmem(), hbm()],
        out_specs=(hbm(), hbm()),
        scratch_shapes=[
            pltpu.SMEM(neighbours.shape, jnp.int32),
            pltpu.SMEM(leaf_counts.shape, jnp.int32),
            pltpu.VMEM((3, leaves, per_leaf), f32),
            pltpu.VMEM((table * 16, per_leaf), f32),
            pltpu.VMEM((table * 16, per_leaf), f32),
            pltpu.VMEM((table * 16, per_leaf), bf16),
            pltpu.VMEM((table * 48, per_leaf), bf16),
            pltpu.VMEM((leaves * 32, per_leaf), f32),
            pltpu.VMEM((leaves * per_leaf, 32), bf16),
            pltpu.VMEM((16 * leaves, per_leaf), f32),
            pltpu.VMEM(m2l_sources.shape, jnp.int32),
            pltpu.VMEM(m2l_ops.shape, bf16),
            pltpu.VMEM((picks, owned), bf16),
            pltpu.VMEM((picks, tile), bf16),
            pltpu.VMEM((coeffs, owned), bf16),
            pltpu.SemaphoreType.DMA((steps + 4,)),
            pltpu.SemaphoreType.DMA((-(-coeffs // (2 * lanes)),)),
        ],
        compiler_params=pltpu.CompilerParams(vmem_limit_bytes=40 * 2**20),
        name="fields",
    )(neighbours, leaf_counts, packed, odd, even, in_hbm(m2l_sources), arrived, in_hbm(m2l_ops))


def call_presum(hx_count, partial_multipoles, shared_slots, positions, forces, leaf_counts, neighbours):
    row_count, coeffs = partial_multipoles.shape[1:]
    cap = row_count // hx_count
    uniq = cap // 4
    slot_count = hx_count * uniq
    width = -(-(coeffs + 2) // lanes) * lanes
    tile = width
    steps = -(-coeffs // tile)
    leaves = leaf_counts.shape[1]
    per_leaf = positions.shape[2] // leaves

    return pl.pallas_call(
        functools.partial(presum_kernel, cap, uniq, tile),
        out_shape=(
            jax.ShapeDtypeStruct((slot_count, width), bf16),
            pltpu.VMEM((6, leaves, per_leaf), f32),
            pltpu.VMEM(leaf_counts.shape, jnp.int32),
            pltpu.VMEM(neighbours.shape, jnp.int32),
        ),
        in_specs=[hbm()] * 6,
        out_specs=(hbm(), vmem(), vmem(), vmem()),
        scratch_shapes=[
            pltpu.SMEM(leaf_counts.shape, jnp.int32),
            pltpu.VMEM(shared_slots.shape, jnp.int32),
            pltpu.VMEM((coeffs, row_count), bf16),
            pltpu.VMEM((3, leaves, per_leaf), f32),
            pltpu.VMEM((3, leaves, per_leaf), f32),
            pltpu.VMEM((slot_count, width), bf16),
            pltpu.SemaphoreType.DMA((6,)),
            pltpu.SemaphoreType.DMA((steps,)),
            pltpu.SemaphoreType.DMA((steps,)),
        ],
        compiler_params=pltpu.CompilerParams(vmem_limit_bytes=16 * 2**20),
        name="presum",
    )(
        *map(
            in_hbm,
            (
                leaf_counts,
                shared_slots,
                partial_multipoles[0].T,
                positions[0].reshape(3, leaves, per_leaf),
                forces[0].reshape(3, leaves, per_leaf),
                neighbours,
            ),
        )
    )


def on_device(
    partial_multipoles,
    shared_slots,
    m2l_sources,
    m2l_ops,
    positions,
    forces,
    leaf_counts,
    neighbours,
):
    hx_count, nb_count = lax.axis_size("hx"), lax.axis_size("nb")
    sums, packed, counts, sources = call_presum(
        hx_count, partial_multipoles, shared_slots, positions, forces, leaf_counts, neighbours
    )

    even_pairs = [(i, i + 1) for i in range(0, nb_count - 1, 2)]
    odd_pairs = [(i, i + 1) for i in range(1, nb_count - 1, 2)]
    odd = lax.ppermute(packed, "nb", odd_pairs + [(j, i) for i, j in odd_pairs])
    even = lax.ppermute(packed, "nb", even_pairs + [(j, i) for i, j in even_pairs])
    arrived = lax.all_to_all(
        sums.reshape(hx_count, -1, sums.shape[1]), "hx", split_axis=0, concat_axis=0, tiled=True
    ).reshape(sums.shape)

    velocity, local = call_fields(sources, counts, packed, even, odd, m2l_sources, arrived, m2l_ops)

    return local.T[None], velocity.reshape(positions.shape)


def solution(mesh):
    placed = (
        P("nb", "hx", None),
        P("nb", "hx"),
        P("nb", None, "hx"),
        P(),
        P("nb", None, "hx"),
        P("nb", None, "hx"),
        P("nb", "hx"),
        P("nb", None, "hx"),
    )
    return jax.shard_map(
        on_device,
        mesh=mesh,
        in_specs=placed,
        out_specs=(P("nb", "hx", None), P("nb", None, "hx")),
        check_vma=False,
    )
```

time: 28.8 us -> 25.5 us (0.89)
  Pallas kernels: 16.2 us -> 11.1 us
  waiting for transfers between devices: 1.4 us -> 6.1 us
  starting transfers between devices: 10.3 us -> 7.41 us
    pallas_call x3 -> x2, Pallas kernels: 16.2 us -> 11.1 us  [the longest x1 8.24 us: call_fields(): pl.pallas_call(functools.partial(fields_kernel, 'nb'), out_shape=(jax.Sha...]
    ppermute x1, starting transfers between devices: 5.9 us -> 1.58 us  [on_device(): lax.ppermute(packed, 'nb', even_pairs + [(j, i) for i, j in even_pairs])]
    all_to_all x1, waiting for transfers between devices: 1.4 us -> 4.18 us  [on_device(): lax.all_to_all(sums.reshape(hx_count, -1, sums.shape[1]), 'hx', split_axi...]
    ppermute x1, waiting for transfers between devices: 0.01 us -> 1.92 us  [on_device(): lax.ppermute(packed, 'nb', even_pairs + [(j, i) for i, j in even_pairs])]
    all_to_all x1, starting transfers between devices: 3.73 us -> 5.18 us  [on_device(): lax.all_to_all(sums.reshape(hx_count, -1, sums.shape[1]), 'hx', split_axi...]
  transfers between devices with their start and end apart: 3 -> 3, of which waited for: 1 -> 2; matrix products, arithmetic and copies ran while one was open for 0% -> 0% of each run, Pallas kernels for 24% -> 0%
where the time goes in v2:
time: 25.5 us; the launch traced here: 25.3 us
  Pallas kernels  11.1 us (44%)
  starting transfers between devices  7.41 us (29%)
  waiting for transfers between devices  6.1 us (24%)
  between operations  0.65 us (3%)
    pallas_call x1, Pallas kernels, call_fields(): pl.pallas_call(functools.partial(fields_kernel, 'nb'), out_shape=(jax.Sha...  8.24 us
    all_to_all x1, starting transfers between devices, on_device(): lax.all_to_all(sums.reshape(hx_count, -1, sums.shape[1]), 'hx', split_axi...  5.18 us
    all_to_all x1, waiting for transfers between devices, on_device(): lax.all_to_all(sums.reshape(hx_count, -1, sums.shape[1]), 'hx', split_axi...  4.18 us
    pallas_call x1, Pallas kernels, call_presum(): pl.pallas_call(functools.partial(presum_kernel, cap, uniq, tile), out_sha...  2.89 us
    ppermute x1, waiting for transfers between devices, on_device(): lax.ppermute(packed, 'nb', even_pairs + [(j, i) for i, j in even_pairs])  1.92 us
    ppermute x1, starting transfers between devices, on_device(): lax.ppermute(packed, 'nb', even_pairs + [(j, i) for i, j in even_pairs])  1.58 us
    ppermute x1, starting transfers between devices, on_device(): odd = lax.ppermute(packed, 'nb', odd_pairs + [(j, i) for i, j in odd_pairs])  0.65 us
  transfers between devices with their start and end apart: 3, of which 2 were waited for; matrix products, arithmetic and copies ran while one was open for 0% of the time, Pallas kernels for 0%

profile of v2, /device:TPU:0, one launch (start us, length us, event | category | flops | bytes accessed | tf_op | source)
XLA Modules:
  0.0 25.3 jit_solution(16744513719297101539)
XLA Ops:
  0.6 2.9 %presum.1 = (bf16[128,1536]{1,0:T(8,128)(2,1)}, f32[6,16,128]{2,1,0:T(8,128)S(1)}, s32[1,16]{1,0:T(1,128)S(1)}, s32[1,8,16]{2,1,0:T(8,128)S(1)}) custom-call(s32[1,16]{1,0:T(1,128)} %counts_hbm.1, s32[1,512]{1,0:T(1,128)} %slots_hbm.1, bf16[1464,512]{1,0:T(8,128)(2,1)} %bitcast.12, f32[3,16,128]{2,1,0:T(8,128)} %bitcast.13, f32[3,16,128]{2,1,0:T(8,128)} %bitcast.14, ...), custom_call_target="tpu_custom_call" | custom-call | tf_op jit(solution)/shard_map/presum/pallas_call | solution.py:342
  3.5 5.2 %all-to-all-start = ((bf16[8,16,1536]{2,1,0:T(8,128)(2,1)}), bf16[8,16,1536]{2,1,0:T(8,128)(2,1)S(1)}, u32[]{:S(2)}, u32[]{:S(2)}) async-start(bf16[8,16,1536]{2,1,0:T(8,128)(2,1)} %bitcast.4), calls=%async_computation | async-start | bytes 786432 | tf_op jit(solution)/shard_map/all_to_all | solution.py:399
  8.7 1.6 %collective-permute-start.1 = (f32[6,16,128]{2,1,0:T(8,128)S(1)}, f32[6,16,128]{2,1,0:T(8,128)S(1)}, u32[]{:S(2)}, u32[]{:S(2)}) collective-permute-start(f32[6,16,128]{2,1,0:T(8,128)S(1)} %get-tuple-element.10.own_ref), channel_id=1, source_target_pairs={{0,1},{2,3},{1,0},{3,2},{4,5},{6,7},{5,4},{7,6},{8,9},{10,11},{9,8... | collective-permute-start | bytes 147464 | tf_op jit(solution)/shard_map/ppermute | solution.py:398
  10.3 0.7 %collective-permute-start = (f32[6,16,128]{2,1,0:T(8,128)S(1)}, f32[6,16,128]{2,1,0:T(8,128)S(1)}, u32[]{:S(2)}, u32[]{:S(2)}) collective-permute-start(f32[6,16,128]{2,1,0:T(8,128)S(1)} %get-tuple-element.10.own_ref), channel_id=1, source_target_pairs={{1,2},{2,1},{5,6},{6,5},{9,10},{10,9},{13,14},{14,13},{17,18},{18,... | collective-permute-start | bytes 147464 | tf_op jit(solution)/shard_map/ppermute | solution.py:397
  10.9 1.9 %collective-permute-done.1.even_ref = f32[6,16,128]{2,1,0:T(8,128)S(1)} collective-permute-done((f32[6,16,128]{2,1,0:T(8,128)S(1)}, f32[6,16,128]{2,1,0:T(8,128)S(1)}, u32[]{:S(2)}, u32[]{:S(2)}) %collective-permute-start.1) | collective-permute-done | bytes 49184 | tf_op jit(solution)/shard_map/ppermute | solution.py:398
  12.9 0.0 collective-permute-done.odd_ref
  12.9 4.2 %all-to-all-done = bf16[8,16,1536]{2,1,0:T(8,128)(2,1)S(1)} async-done(((bf16[8,16,1536]{2,1,0:T(8,128)(2,1)}), bf16[8,16,1536]{2,1,0:T(8,128)(2,1)S(1)}, u32[]{:S(2)}, u32[]{:S(2)}) %all-to-all-start) | async-done | bytes 393248 | tf_op jit(solution)/shard_map/all_to_all | solution.py:399
  17.1 8.2 %fields.1 = (f32[3,16,128]{2,1,0:T(8,128)}, bf16[1464,1024]{1,0:T(8,128)(2,1)}) custom-call(s32[1,8,16]{2,1,0:T(8,128)S(1)} %get-tuple-element.8.neighbours_vmem, s32[1,16]{1,0:T(1,128)S(1)} %get-tuple-element.9.counts_vmem, f32[6,16,128]{2,1,0:T(8,128)S(1)} %get-tuple-element.10.own_ref, f32[6,16,128]{2,1,0:T(8,128)S(1)} %collective-permute-done.odd_ref, ...), custom_call_target="tpu_custom_call" | custom-call | tf_op jit(solution)/shard_map/fields/pallas_call | solution.py:299
Async XLA Ops:
  3.5 13.5 %all-to-all-start = ((bf16[8,16,1536]{2,1,0:T(8,128)(2,1)}), bf16[8,16,1536]{2,1,0:T(8,128)(2,1)S(1)}, u32[]{:S(2)}, u32[]{:S(2)}) async-start(bf16[8,16,1536]{2,1,0:T(8,128)(2,1)} %bitcast.4), calls=%async_computation | async-start | bytes 786432 | tf_op jit(solution)/shard_map/all_to_all | solution.py:399
  8.7 4.2 %collective-permute-start.1 = (f32[6,16,128]{2,1,0:T(8,128)S(1)}, f32[6,16,128]{2,1,0:T(8,128)S(1)}, u32[]{:S(2)}, u32[]{:S(2)}) collective-permute-start(f32[6,16,128]{2,1,0:T(8,128)S(1)} %get-tuple-element.10.own_ref), channel_id=1, source_target_pairs={{0,1},{2,3},{1,0},{3,2},{4,5},{6,7},{5,4},{7,6},{8,9},{10,11},{9,8... | collective-permute-start | bytes 147464 | tf_op jit(solution)/shard_map/ppermute | solution.py:398
  10.3 2.6 %collective-permute-start = (f32[6,16,128]{2,1,0:T(8,128)S(1)}, f32[6,16,128]{2,1,0:T(8,128)S(1)}, u32[]{:S(2)}, u32[]{:S(2)}) collective-permute-start(f32[6,16,128]{2,1,0:T(8,128)S(1)} %get-tuple-element.10.own_ref), channel_id=1, source_target_pairs={{1,2},{2,1},{5,6},{6,5},{9,10},{10,9},{13,14},{14,13},{17,18},{18,... | collective-permute-start | bytes 147464 | tf_op jit(solution)/shard_map/ppermute | solution.py:397

commit v3 on v2

--- a/solution.py
+++ b/solution.py
@@ -27,7 +27,7 @@
 
 def presum_kernel(
     cap, uniq, tile, counts_hbm, slots_hbm, rows_hbm, pos_hbm, frc_hbm, neighbours_hbm,
-    sums_hbm, packed_ref, counts_out, neighbours_out,
+    sums_hbm, packed_ref, live_ref, neighbours_out,
     counts_ref, slots_ref, rows_ref, pos_ref, frc_ref, sums_ref, arrival, rows_sem, sums_sem,
 ):
     coeffs, row_count = rows_ref.shape
@@ -38,7 +38,6 @@
         (counts_hbm, counts_ref),
         (pos_hbm, pos_ref),
         (frc_hbm, frc_ref),
-        (counts_hbm, counts_out),
         (neighbours_hbm, neighbours_out),
     )
     copies = [pltpu.make_async_copy(a, b, arrival.at[i]) for i, (a, b) in enumerate(pairs)]
@@ -92,12 +91,12 @@
     for copy in copies[1:]:
         copy.wait()
     leaves, per_leaf = pos_ref.shape[1:]
-    leaf_at = lax.broadcasted_iota(jnp.int32, (leaves, per_leaf), 0)
+    blank = jnp.zeros((1, lanes - leaves), jnp.int32)
+    count = jnp.concatenate([counts_ref[...], blank], axis=1)
+    count = jnp.broadcast_to(count, (lanes, lanes)).T[:leaves]
     point_at = lax.broadcasted_iota(jnp.int32, (leaves, per_leaf), 1)
-    count = jnp.zeros((leaves, per_leaf), jnp.int32)
-    for leaf in range(leaves):
-        count = jnp.where(leaf_at == leaf, counts_ref[0, leaf], count)
-    live = (point_at < count).astype(f32)
+    live = jnp.where(point_at < count, 1.0, 0.0)
+    live_ref[...] = live
     for axis in range(3):
         packed_ref[axis] = pos_ref[axis]
         packed_ref[3 + axis] = frc_ref[axis] * live
@@ -106,8 +105,8 @@
 
 
 def near_field(
-    slab_axis, lists, neighbours_ref, counts_ref, own_ref, even_ref, odd_ref, out_ref,
-    point_ref, moment_ref, source_ref, weight_ref, target_wide_ref, target_ref, sums_ref,
+    slab_axis, neighbours_ref, live_ref, own_ref, even_ref, odd_ref, out_ref,
+    point_ref, moment_ref, source_ref, weight_ref, target_wide_ref, target_ref, sums_ref, cube_ref,
 ):
     _, leaves, per_leaf = own_ref.shape
     group = 16
@@ -150,64 +149,81 @@
     stored(target_wide_ref, 0, 2 * group, rows)
 
     row_at = lax.broadcasted_iota(jnp.int32, (group, per_leaf), 0)
-    for leaf in range(3 * leaves):
-        at = pl.ds(leaf * group, group)
+    def convert(leaf, carry):
+        at = pl.ds(pl.multiple_of(leaf * group, group), group)
         point = jnp.where(row_at < 9, point_ref[at, :], jnp.where(row_at < 12, 1.0, 0.0))
         source_ref[at, :] = point.astype(bf16)
         moment = jnp.where(row_at < 15, moment_ref[at, :], 0.0)
         for i, piece in enumerate(split(moment, pieces)):
-            weight_ref[pl.ds((leaf * pieces + i) * group, group), :] = piece.astype(bf16)
-    for leaf in range(leaves):
-        block = target_wide_ref[pl.ds(leaf * 2 * group, 2 * group), :]
-        target_ref[pl.ds(leaf * per_leaf, per_leaf), :] = block.T.astype(bf16)
-
-    for copy in lists:
-        copy.wait()
-
-    def one_leaf(leaf, carry):
-        target = target_ref[pl.ds(pl.multiple_of(leaf * per_leaf, per_leaf), per_leaf), :]
-        total = jnp.zeros((per_leaf, pieces * group), f32)
-        for n in range(0, nbr_count, 2):
-            near = [neighbours_ref[0, n + k, leaf] for k in range(2)]
-            points = [source_ref[pl.ds(pl.multiple_of(s * group, group), group), :] for s in near]
-            deep = pieces * group
-            weights = [weight_ref[pl.ds(pl.multiple_of(s * deep, group), deep), :] for s in near]
-            points = jnp.concatenate(points, axis=1)
-            dist_sq = jnp.dot(
-                target, jnp.concatenate([points, points], axis=0), preferred_element_type=f32
-            )
-            inverse = lax.rsqrt(dist_sq)
-            cube = (inverse * inverse * inverse).astype(bf16)
-            total = total + lax.dot_general(
-                cube,
+            to = pl.ds(pl.multiple_of((leaf * pieces + i) * group, group), group)
+            weight_ref[to, :] = piece.astype(bf16)
+        return carry
+
+    def turn(leaf, carry):
+        block = target_wide_ref[pl.ds(pl.multiple_of(leaf * 2 * group, group), 2 * group), :]
+        to = pl.ds(pl.multiple_of(leaf * per_leaf, per_leaf), per_leaf)
+        target_ref[to, :] = block.T.astype(bf16)
+        return carry
+
+    lax.fori_loop(0, 3 * leaves, convert, 0, unroll=8)
+    lax.fori_loop(0, leaves, turn, 0, unroll=8)
+
+    deep = pieces * group
+    batch = cube_ref.shape[0] // 2
+
+    def cubes(step):
+        slot = lax.rem(step, 2) * batch
+        for k in range(batch):
+            leaf = step * batch + k
+            target = target_ref[pl.ds(pl.multiple_of(leaf * per_leaf, per_leaf), per_leaf), :]
+            for n in range(0, nbr_count, 2):
+                near = [neighbours_ref[0, n + i, leaf] for i in range(2)]
+                points = [source_ref[pl.ds(pl.multiple_of(i * group, group), group), :] for i in near]
+                points = jnp.concatenate(points, axis=1)
+                dist_sq = jnp.dot(
+                    target, jnp.concatenate([points, points], axis=0), preferred_element_type=f32
+                )
+                inverse = lax.rsqrt(dist_sq)
+                cube = (inverse * inverse * inverse).astype(bf16)
+                cube_ref[slot + k, :, n * per_leaf : (n + 2) * per_leaf] = cube
+
+    def sums(step):
+        slot = lax.rem(step, 2) * batch
+        for k in range(batch):
+            leaf = step * batch + k
+            near = [neighbours_ref[0, n, leaf] for n in range(nbr_count)]
+            weights = [weight_ref[pl.ds(pl.multiple_of(i * deep, group), deep), :] for i in near]
+            total = lax.dot_general(
+                cube_ref[slot + k],
                 jnp.concatenate(weights, axis=1),
                 (((1,), (1,)), ((), ())),
                 preferred_element_type=f32,
-            )
-        turned = total.T
-        sums = turned[:group] + turned[group : 2 * group] + turned[2 * group :]
-        sums_ref[pl.ds(leaf, group, stride=leaves), :] = sums
+            ).T
+            total = total[:group] + total[group : 2 * group] + total[2 * group :]
+            sums_ref[pl.ds(leaf, group, stride=leaves), :] = total
+
+    def both(step, carry):
+        sums(step - 1)
+        cubes(step)
         return carry
 
-    lax.fori_loop(0, leaves, one_leaf, 0, unroll=8)
+    steps = leaves // batch
+    cubes(0)
+    lax.fori_loop(1, steps, both, 0)
+    sums(steps - 1)
 
     got = [sums_ref[pl.ds(row * leaves, leaves), :] for row in range(15)]
     first, mixed, rest = got[:3], [got[3 + 3 * i : 6 + 3 * i] for i in range(3)], got[12:]
-    leaf_at = lax.broadcasted_iota(jnp.int32, (leaves, per_leaf), 0)
-    point_at = lax.broadcasted_iota(jnp.int32, (leaves, per_leaf), 1)
-    count = jnp.zeros((leaves, per_leaf), jnp.int32)
-    for leaf in range(leaves):
-        count = jnp.where(leaf_at == leaf, counts_ref[0, leaf], count)
-    factor = jnp.where(point_at < count, inv_eight_pi, 0.0)
+    factor = live_ref[...] * inv_eight_pi
     shift = dot3(own_place, first) - (mixed[0][0] + mixed[1][1] + mixed[2][2])
     for i in range(3):
         turned = dot3(own_place, [2.0 * mixed[i][j] + mixed[j][i] for j in range(3)])
         out_ref[i] = (own_norm * first[i] + own_place[i] * shift - turned + rest[i]) * factor
 
 
-def far_field(sources_ref, rows_ref, ops_ref, out_ref, out_hbm, pick_ref, moved_ref, out_sem, ready):
-    directions, coeffs, _ = ops_ref.shape
-    slot_count = rows_ref.shape[0]
+def far_field(sources_ref, rows_ref, tile_of, out_ref, out_hbm, pick_ref, moved_ref, out_sem):
+    coeffs, slot_count = out_ref.shape[0], rows_ref.shape[0]
+    directions = pick_ref.shape[0] // slot_count
     tile = moved_ref.shape[1]
     octant = rows_ref[:, coeffs : coeffs + 2].astype(f32).astype(jnp.int32)
     octant = octant[:, :1] * id_base + octant[:, 1:]
@@ -217,10 +233,10 @@
     rows = rows_ref[:, :coeffs]
     stores = []
     for i, start in enumerate(range(0, coeffs, tile)):
-        ready(i)
+        ops_ref = tile_of(i)
         size = min(tile, coeffs - start)
         for t in range(directions):
-            moved = jnp.dot(rows, ops_ref[t, :, start : start + size], preferred_element_type=f32)
+            moved = jnp.dot(rows, ops_ref[t], preferred_element_type=f32)
             moved_ref[t * slot_count : (t + 1) * slot_count, :size] = moved.astype(bf16)
         for low in range(0, size, 2 * lanes):
             rest = min(2 * lanes, size - low)
@@ -238,39 +254,41 @@
     return stores
 
 
-def fields_kernel(
-    slab_axis, neighbours_vmem, counts_vmem, own_ref, odd_ref, even_ref, picks_hbm, rows_ref, ops_hbm,
-    velocity_hbm, local_hbm,
-    neighbours_ref, counts_ref, velocity_ref,
-    point_ref, moment_ref, source_ref, weight_ref, target_wide_ref, target_ref, sums_ref,
-    picks_ref, ops_ref, pick_ref, moved_ref, local_ref, ops_sem, out_sem,
+def near_kernel(
+    slab_axis, neighbours_ref, live_ref, own_ref, odd_ref, even_ref, ops_hbm,
+    velocity_ref, head_ref,
+    point_ref, moment_ref, source_ref, weight_ref, target_wide_ref, target_ref, sums_ref, cube_ref, sem,
+):
+    head = pltpu.make_async_copy(ops_hbm.at[:, :, pl.ds(0, head_ref.shape[2])], head_ref, sem)
+    head.start()
+    near_field(
+        slab_axis, neighbours_ref, live_ref, own_ref, even_ref, odd_ref, velocity_ref,
+        point_ref, moment_ref, source_ref, weight_ref, target_wide_ref, target_ref, sums_ref, cube_ref,
+    )
+    head.wait()
+
+
+def far_kernel(
+    picks_ref, rows_ref, head_ref, velocity_ref, ops_hbm, local_hbm, velocity_hbm,
+    ops_ref, pick_ref, moved_ref, local_ref, ops_sem, out_sem,
 ):
     coeffs, tile = ops_hbm.shape[1], moved_ref.shape[1]
-    steps = -(-coeffs // tile)
-    lists = (
-        pltpu.make_async_copy(neighbours_vmem, neighbours_ref, ops_sem.at[steps + 1]),
-        pltpu.make_async_copy(counts_vmem, counts_ref, ops_sem.at[steps + 2]),
-    )
-    for copy in lists:
-        copy.start()
-    picks_load = pltpu.make_async_copy(picks_hbm, picks_ref, ops_sem.at[steps])
-    picks_load.start()
-    loads = []
-    for i, start in enumerate(range(0, coeffs, tile)):
+    loads = [None]
+    for i, start in enumerate(range(tile, coeffs, tile)):
         at = pl.ds(start, min(tile, coeffs - start))
         loads.append(pltpu.make_async_copy(ops_hbm.at[:, :, at], ops_ref.at[:, :, at], ops_sem.at[i]))
         loads[-1].start()
-    near_field(
-        slab_axis, lists, neighbours_ref, counts_ref, own_ref, even_ref, odd_ref, velocity_ref,
-        point_ref, moment_ref, source_ref, weight_ref, target_wide_ref, target_ref, sums_ref,
-    )
-    velocity_store = pltpu.make_async_copy(velocity_ref, velocity_hbm, ops_sem.at[steps + 3])
+
+    velocity_store = pltpu.make_async_copy(velocity_ref, velocity_hbm, ops_sem.at[len(loads) - 1])
     velocity_store.start()
-    picks_load.wait()
-    stores = far_field(
-        picks_ref, rows_ref, ops_ref, local_ref, local_hbm, pick_ref, moved_ref, out_sem,
-        lambda i: loads[i].wait(),
-    )
+
+    def tile_of(i):
+        if i == 0:
+            return head_ref
+        loads[i].wait()
+        return ops_ref.at[:, :, pl.ds(i * tile, min(tile, coeffs - i * tile))]
+
+    stores = far_field(picks_ref, rows_ref, tile_of, local_ref, local_hbm, pick_ref, moved_ref, out_sem)
     for store in stores + [velocity_store]:
         store.wait()
 
@@ -283,31 +301,27 @@
     return pltpu.with_memory_space_constraint(array, pltpu.HBM)
 
 
+def smem():
+    return pl.BlockSpec(memory_space=pltpu.SMEM)
+
+
 def hbm():
     return pl.BlockSpec(memory_space=pltpu.HBM)
 
 
-def call_fields(neighbours, leaf_counts, packed, even, odd, m2l_sources, arrived, m2l_ops):
+def call_near(neighbours, live, packed, odd, even, m2l_ops, tile):
     _, leaves, per_leaf = packed.shape
     directions, coeffs, _ = m2l_ops.shape
-    owned = m2l_sources.shape[2]
-    slot_count = arrived.shape[0]
-    tile = 4 * lanes
-    steps = -(-coeffs // tile)
     table = 3 * leaves
-    picks = directions * slot_count
     return pl.pallas_call(
-        functools.partial(fields_kernel, "nb"),
+        functools.partial(near_kernel, "nb"),
         out_shape=(
-            jax.ShapeDtypeStruct((3, leaves, per_leaf), f32),
-            jax.ShapeDtypeStruct((coeffs, owned), bf16),
+            pltpu.VMEM((3, leaves, per_leaf), f32),
+            pltpu.VMEM((directions, coeffs, tile), bf16),
         ),
-        in_specs=[vmem(), vmem(), vmem(), vmem(), vmem(), hbm(), vmem(), hbm()],
-        out_specs=(hbm(), hbm()),
+        in_specs=[smem()] + [vmem()] * 4 + [hbm()],
+        out_specs=(vmem(), vmem()),
         scratch_shapes=[
-            pltpu.SMEM(neighbours.shape, jnp.int32),
-            pltpu.SMEM(leaf_counts.shape, jnp.int32),
-            pltpu.VMEM((3, leaves, per_leaf), f32),
             pltpu.VMEM((table * 16, per_leaf), f32),
             pltpu.VMEM((table * 16, per_leaf), f32),
             pltpu.VMEM((table * 16, per_leaf), bf16),
@@ -315,17 +329,37 @@
             pltpu.VMEM((leaves * 32, per_leaf), f32),
             pltpu.VMEM((leaves * per_leaf, 32), bf16),
             pltpu.VMEM((16 * leaves, per_leaf), f32),
-            pltpu.VMEM(m2l_sources.shape, jnp.int32),
+            pltpu.VMEM((2 * 8, per_leaf, neighbours.shape[1] * per_leaf), bf16),
+            pltpu.SemaphoreType.DMA,
+        ],
+        compiler_params=pltpu.CompilerParams(vmem_limit_bytes=24 * 2**20),
+        name="near",
+    )(neighbours, live, packed, odd, even, in_hbm(m2l_ops))
+
+
+def call_far(m2l_sources, arrived, head, velocity, m2l_ops):
+    directions, coeffs, tile = head.shape
+    owned = m2l_sources.shape[2]
+    picks = directions * arrived.shape[0]
+    return pl.pallas_call(
+        far_kernel,
+        out_shape=(
+            jax.ShapeDtypeStruct((coeffs, owned), bf16),
+            jax.ShapeDtypeStruct(velocity.shape, f32),
+        ),
+        in_specs=[vmem()] * 4 + [hbm()],
+        out_specs=(hbm(), hbm()),
+        scratch_shapes=[
             pltpu.VMEM(m2l_ops.shape, bf16),
             pltpu.VMEM((picks, owned), bf16),
             pltpu.VMEM((picks, tile), bf16),
             pltpu.VMEM((coeffs, owned), bf16),
-            pltpu.SemaphoreType.DMA((steps + 4,)),
+            pltpu.SemaphoreType.DMA((-(-coeffs // tile),)),
             pltpu.SemaphoreType.DMA((-(-coeffs // (2 * lanes)),)),
         ],
         compiler_params=pltpu.CompilerParams(vmem_limit_bytes=40 * 2**20),
-        name="fields",
-    )(neighbours, leaf_counts, packed, odd, even, in_hbm(m2l_sources), arrived, in_hbm(m2l_ops))
+        name="far",
+    )(m2l_sources, arrived, head, velocity, in_hbm(m2l_ops))
 
 
 def call_presum(hx_count, partial_multipoles, shared_slots, positions, forces, leaf_counts, neighbours):
@@ -344,19 +378,19 @@
         out_shape=(
             jax.ShapeDtypeStruct((slot_count, width), bf16),
             pltpu.VMEM((6, leaves, per_leaf), f32),
-            pltpu.VMEM(leaf_counts.shape, jnp.int32),
-            pltpu.VMEM(neighbours.shape, jnp.int32),
+            pltpu.VMEM((leaves, per_leaf), f32),
+            pltpu.SMEM(neighbours.shape, jnp.int32),
         ),
         in_specs=[hbm()] * 6,
-        out_specs=(hbm(), vmem(), vmem(), vmem()),
+        out_specs=(hbm(), vmem(), vmem(), smem()),
         scratch_shapes=[
-            pltpu.SMEM(leaf_counts.shape, jnp.int32),
+            pltpu.VMEM(leaf_counts.shape, jnp.int32),
             pltpu.VMEM(shared_slots.shape, jnp.int32),
             pltpu.VMEM((coeffs, row_count), bf16),
             pltpu.VMEM((3, leaves, per_leaf), f32),
             pltpu.VMEM((3, leaves, per_leaf), f32),
             pltpu.VMEM((slot_count, width), bf16),
-            pltpu.SemaphoreType.DMA((6,)),
+            pltpu.SemaphoreType.DMA((5,)),
             pltpu.SemaphoreType.DMA((steps,)),
             pltpu.SemaphoreType.DMA((steps,)),
         ],
@@ -388,19 +422,20 @@
     neighbours,
 ):
     hx_count, nb_count = lax.axis_size("hx"), lax.axis_size("nb")
-    sums, packed, counts, sources = call_presum(
+    sums, packed, live, sources = call_presum(
         hx_count, partial_multipoles, shared_slots, positions, forces, leaf_counts, neighbours
     )
 
     even_pairs = [(i, i + 1) for i in range(0, nb_count - 1, 2)]
     odd_pairs = [(i, i + 1) for i in range(1, nb_count - 1, 2)]
+    even = lax.ppermute(packed, "nb", even_pairs + [(j, i) for i, j in even_pairs])
     odd = lax.ppermute(packed, "nb", odd_pairs + [(j, i) for i, j in odd_pairs])
-    even = lax.ppermute(packed, "nb", even_pairs + [(j, i) for i, j in even_pairs])
     arrived = lax.all_to_all(
         sums.reshape(hx_count, -1, sums.shape[1]), "hx", split_axis=0, concat_axis=0, tiled=True
     ).reshape(sums.shape)
 
-    velocity, local = call_fields(sources, counts, packed, even, odd, m2l_sources, arrived, m2l_ops)
+    velocity, head = call_near(sources, live, packed, odd, even, m2l_ops, 4 * lanes)
+    local, velocity = call_far(m2l_sources, arrived, head, velocity, m2l_ops)
 
     return local.T[None], velocity.reshape(positions.shape)
 

time: 25.5 us -> 24 us (0.941)
  the two profiles are of different devices: /device:TPU:0 before, /device:TPU:18 now
where the time goes in v3:
time: 24 us; the launch traced here: 23.8 us
  Pallas kernels  11.3 us (47%)
  starting transfers between devices  7.75 us (32%)
  waiting for transfers between devices  4.06 us (17%)
  between operations  0.67 us (3%)
    pallas_call x1, Pallas kernels, call_far(): pl.pallas_call(far_kernel, out_shape=(jax.ShapeDtypeStruct((coeffs, owned...  5.07 us
    all_to_all x1, starting transfers between devices, on_device(): lax.all_to_all(sums.reshape(hx_count, -1, sums.shape[1]), 'hx', split_axi...  4.26 us
    ppermute x1, waiting for transfers between devices, on_device(): odd = lax.ppermute(packed, 'nb', odd_pairs + [(j, i) for i, j in odd_pairs])  3.46 us
    pallas_call x1, Pallas kernels, call_near(): pl.pallas_call(functools.partial(near_kernel, 'nb'), out_shape=(pltpu.VME...  3.35 us
    pallas_call x1, Pallas kernels, call_presum(): pl.pallas_call(functools.partial(presum_kernel, cap, uniq, tile), out_sha...  2.88 us
    ppermute x1, starting transfers between devices, on_device(): odd = lax.ppermute(packed, 'nb', odd_pairs + [(j, i) for i, j in odd_pairs])  1.91 us
    ppermute x1, starting transfers between devices, on_device(): lax.ppermute(packed, 'nb', even_pairs + [(j, i) for i, j in even_pairs])  1.58 us
    ppermute x1, waiting for transfers between devices, on_device(): lax.ppermute(packed, 'nb', even_pairs + [(j, i) for i, j in even_pairs])  0.59 us
  transfers between devices with their start and end apart: 3, of which 2 were waited for; matrix products, arithmetic and copies ran while one was open for 0% of the time, Pallas kernels for 14%

profile of v3, /device:TPU:18, one launch (start us, length us, event | category | flops | bytes accessed | tf_op | source)
XLA Modules:
  0.0 23.8 jit_solution(2745568968062147304)
XLA Ops:
  0.6 2.9 %presum.1 = (bf16[128,1536]{1,0:T(8,128)(2,1)}, f32[6,16,128]{2,1,0:T(8,128)S(1)}, f32[16,128]{1,0:T(8,128)S(1)}, s32[1,8,16]{2,1,0:T(8,128)S(4)}) custom-call(s32[1,16]{1,0:T(1,128)} %counts_hbm.1, s32[1,512]{1,0:T(1,128)} %slots_hbm.1, bf16[1464,512]{1,0:T(8,128)(2,1)} %bitcast.12, f32[3,16,128]{2,1,0:T(8,128)} %bitcast.13, f32[3,16,128]{2,1,0:T(8,128)} %bitcast.14, ...), custom_call_target="tpu_custom_call" | custom-call | tf_op jit(solution)/shard_map/presum/pallas_call | solution.py:376
  3.5 4.3 %all-to-all-start = ((bf16[8,16,1536]{2,1,0:T(8,128)(2,1)}), bf16[8,16,1536]{2,1,0:T(8,128)(2,1)S(1)}, u32[]{:S(2)}, u32[]{:S(2)}) async-start(bf16[8,16,1536]{2,1,0:T(8,128)(2,1)} %bitcast.4), calls=%async_computation | async-start | bytes 786432 | tf_op jit(solution)/shard_map/all_to_all | solution.py:433
  7.8 1.6 %collective-permute-start.1 = (f32[6,16,128]{2,1,0:T(8,128)S(1)}, f32[6,16,128]{2,1,0:T(8,128)S(1)}, u32[]{:S(2)}, u32[]{:S(2)}) collective-permute-start(f32[6,16,128]{2,1,0:T(8,128)S(1)} %get-tuple-element.13.own_ref), channel_id=1, source_target_pairs={{0,1},{2,3},{1,0},{3,2},{4,5},{6,7},{5,4},{7,6},{8,9},{10,11},{9,8... | collective-permute-start | bytes 147464 | tf_op jit(solution)/shard_map/ppermute | solution.py:431
  9.4 1.9 %collective-permute-start = (f32[6,16,128]{2,1,0:T(8,128)S(1)}, f32[6,16,128]{2,1,0:T(8,128)S(1)}, u32[]{:S(2)}, u32[]{:S(2)}) collective-permute-start(f32[6,16,128]{2,1,0:T(8,128)S(1)} %get-tuple-element.13.own_ref), channel_id=1, source_target_pairs={{1,2},{2,1},{5,6},{6,5},{9,10},{10,9},{13,14},{14,13},{17,18},{18,... | collective-permute-start | bytes 147464 | tf_op jit(solution)/shard_map/ppermute | solution.py:432
  11.3 0.6 %collective-permute-done.1.even_ref = f32[6,16,128]{2,1,0:T(8,128)S(1)} collective-permute-done((f32[6,16,128]{2,1,0:T(8,128)S(1)}, f32[6,16,128]{2,1,0:T(8,128)S(1)}, u32[]{:S(2)}, u32[]{:S(2)}) %collective-permute-start.1) | collective-permute-done | bytes 49184 | tf_op jit(solution)/shard_map/ppermute | solution.py:431
  11.9 3.5 %collective-permute-done.odd_ref = f32[6,16,128]{2,1,0:T(8,128)S(1)} collective-permute-done((f32[6,16,128]{2,1,0:T(8,128)S(1)}, f32[6,16,128]{2,1,0:T(8,128)S(1)}, u32[]{:S(2)}, u32[]{:S(2)}) %collective-permute-start) | collective-permute-done | bytes 49184 | tf_op jit(solution)/shard_map/ppermute | solution.py:432
  15.3 0.0 copy-start
  15.3 3.4 %near.1 = (f32[3,16,128]{2,1,0:T(8,128)S(1)}, bf16[2,1464,512]{2,1,0:T(8,128)(2,1)S(1)}) custom-call(s32[1,8,16]{2,1,0:T(8,128)S(4)} %get-tuple-element.11.neighbours_ref, f32[16,128]{1,0:T(8,128)S(1)} %get-tuple-element.12.live_ref, f32[6,16,128]{2,1,0:T(8,128)S(1)} %get-tuple-element.13.own_ref, f32[6,16,128]{2,1,0:T(8,128)S(1)} %collective-permute-done.odd_ref, ...), custom_call_target="tpu_custom_call" | custom-call | tf_op jit(solution)/shard_map/near/pallas_call | solution.py:316
  18.7 0.0 all-to-all-done
  18.7 0.0 copy-done
  18.7 5.1 %far.1 = (bf16[1464,1024]{1,0:T(8,128)(2,1)}, f32[3,16,128]{2,1,0:T(8,128)}) custom-call(s32[1,2,1024]{2,1,0:T(2,128)S(1)} %copy-done, bf16[128,1536]{1,0:T(8,128)(2,1)S(1)} %bitcast.11, bf16[2,1464,512]{2,1,0:T(8,128)(2,1)S(1)} %get-tuple-element.14.head_ref, f32[3,16,128]{2,1,0:T(8,128)S(1)} %get-tuple-element.15.velocity_ref, bf16[2,1464,1464]{2,1,0:T(8,128)(2,1)} %ops_hbm.3), custom_call_target="tpu_custom_call" | custom-call | tf_op jit(solution)/shard_map/far/pallas_call | solution.py:344
Async XLA Ops:
  3.5 15.2 %all-to-all-start = ((bf16[8,16,1536]{2,1,0:T(8,128)(2,1)}), bf16[8,16,1536]{2,1,0:T(8,128)(2,1)S(1)}, u32[]{:S(2)}, u32[]{:S(2)}) async-start(bf16[8,16,1536]{2,1,0:T(8,128)(2,1)} %bitcast.4), calls=%async_computation | async-start | bytes 786432 | tf_op jit(solution)/shard_map/all_to_all | solution.py:433
  7.8 4.1 %collective-permute-start.1 = (f32[6,16,128]{2,1,0:T(8,128)S(1)}, f32[6,16,128]{2,1,0:T(8,128)S(1)}, u32[]{:S(2)}, u32[]{:S(2)}) collective-permute-start(f32[6,16,128]{2,1,0:T(8,128)S(1)} %get-tuple-element.13.own_ref), channel_id=1, source_target_pairs={{0,1},{2,3},{1,0},{3,2},{4,5},{6,7},{5,4},{7,6},{8,9},{10,11},{9,8... | collective-permute-start | bytes 147464 | tf_op jit(solution)/shard_map/ppermute | solution.py:431
  9.4 6.0 %collective-permute-start = (f32[6,16,128]{2,1,0:T(8,128)S(1)}, f32[6,16,128]{2,1,0:T(8,128)S(1)}, u32[]{:S(2)}, u32[]{:S(2)}) collective-permute-start(f32[6,16,128]{2,1,0:T(8,128)S(1)} %get-tuple-element.13.own_ref), channel_id=1, source_target_pairs={{1,2},{2,1},{5,6},{6,5},{9,10},{10,9},{13,14},{14,13},{17,18},{18,... | collective-permute-start | bytes 147464 | tf_op jit(solution)/shard_map/ppermute | solution.py:432
  15.3 3.4 %copy-start = (s32[1,2,1024]{2,1,0:T(2,128)S(1)}, s32[1,2,1024]{2,1,0:T(2,128)}, u32[]{:S(2)}) copy-start(s32[1,2,1024]{2,1,0:T(2,128)} %picks_ref.1) | copy-start | bytes 24580

commit v4 on v3

--- a/solution.py
+++ b/solution.py
@@ -12,6 +12,8 @@
 inv_eight_pi = 1.0 / (8.0 * math.pi)
 id_base = 32
 lanes = 128
+group = 16
+pieces = 3
 bf16 = jnp.bfloat16
 f32 = jnp.float32
 
@@ -104,25 +106,20 @@
         store.wait()
 
 
-def near_field(
-    slab_axis, neighbours_ref, live_ref, own_ref, even_ref, odd_ref, out_ref,
-    point_ref, moment_ref, source_ref, weight_ref, target_wide_ref, target_ref, sums_ref, cube_ref,
+def dot3(left, right):
+    return left[0] * right[0] + left[1] * right[1] + left[2] * right[2]
+
+
+def near_tables(
+    slab_axis, own_ref, even_ref, odd_ref, point_ref, moment_ref, target_wide_ref, source_ref, weight_ref
 ):
     _, leaves, per_leaf = own_ref.shape
-    group = 16
-    pieces = 3
-    nbr_count = neighbours_ref.shape[1]
     even = lax.rem(lax.axis_index(slab_axis), 2) == 0
-    one = jnp.ones((leaves, per_leaf), f32)
 
     def stored(ref, leaf_start, height, rows):
         for row, value in enumerate(rows):
             ref[pl.ds(leaf_start * height + row, leaves, stride=height), :] = value
 
-    def dot3(left, right):
-        return left[0] * right[0] + left[1] * right[1] + left[2] * right[2]
-
-    own_cut = None
     for part in range(3):
         if part == 0:
             comp = [jnp.where(even, odd_ref[c], even_ref[c]) for c in range(6)]
@@ -141,14 +138,14 @@
         moments += [force[i] * (norm + 2.0 * reg_eps2) + along * place[i] for i in range(3)]
         stored(moment_ref, part * leaves, group, moments)
         if part == 1:
-            own_cut, own_norm, own_place = cut, norm, place
-    high = [-2.0 * c[0] for c in own_cut]
-    low = [-2.0 * c[1] for c in own_cut]
-    zero = jnp.zeros_like(one)
-    rows = high + high + [one] * 3 + split(own_norm, 3) + [zero] * 4 + low + low + [zero] * 10
-    stored(target_wide_ref, 0, 2 * group, rows)
+            zero, one = jnp.zeros_like(norm), jnp.ones_like(norm)
+            high = [-2.0 * c[0] for c in cut]
+            low = [-2.0 * c[1] for c in cut]
+            rows = high + high + [one] * 3 + split(norm, 3) + [zero] * 4 + low + low + [zero] * 10
+            stored(target_wide_ref, 0, 2 * group, rows)
 
     row_at = lax.broadcasted_iota(jnp.int32, (group, per_leaf), 0)
+
     def convert(leaf, carry):
         at = pl.ds(pl.multiple_of(leaf * group, group), group)
         point = jnp.where(row_at < 9, point_ref[at, :], jnp.where(row_at < 12, 1.0, 0.0))
@@ -159,66 +156,53 @@
             weight_ref[to, :] = piece.astype(bf16)
         return carry
 
-    def turn(leaf, carry):
-        block = target_wide_ref[pl.ds(pl.multiple_of(leaf * 2 * group, group), 2 * group), :]
-        to = pl.ds(pl.multiple_of(leaf * per_leaf, per_leaf), per_leaf)
-        target_ref[to, :] = block.T.astype(bf16)
-        return carry
-
     lax.fori_loop(0, 3 * leaves, convert, 0, unroll=8)
-    lax.fori_loop(0, leaves, turn, 0, unroll=8)
-
+
+
+def near_leaves(
+    first, neighbours_ref, own_ref, live, target_wide_ref,
+    source_ref, weight_ref, target_ref, cube_ref, sums_ref, out_ref,
+):
+    count, per_leaf = live.shape
+    height = 2 * group
+    nbr_count = neighbours_ref.shape[1]
     deep = pieces * group
-    batch = cube_ref.shape[0] // 2
-
-    def cubes(step):
-        slot = lax.rem(step, 2) * batch
-        for k in range(batch):
-            leaf = step * batch + k
-            target = target_ref[pl.ds(pl.multiple_of(leaf * per_leaf, per_leaf), per_leaf), :]
-            for n in range(0, nbr_count, 2):
-                near = [neighbours_ref[0, n + i, leaf] for i in range(2)]
-                points = [source_ref[pl.ds(pl.multiple_of(i * group, group), group), :] for i in near]
-                points = jnp.concatenate(points, axis=1)
-                dist_sq = jnp.dot(
-                    target, jnp.concatenate([points, points], axis=0), preferred_element_type=f32
-                )
-                inverse = lax.rsqrt(dist_sq)
-                cube = (inverse * inverse * inverse).astype(bf16)
-                cube_ref[slot + k, :, n * per_leaf : (n + 2) * per_leaf] = cube
-
-    def sums(step):
-        slot = lax.rem(step, 2) * batch
-        for k in range(batch):
-            leaf = step * batch + k
-            near = [neighbours_ref[0, n, leaf] for n in range(nbr_count)]
-            weights = [weight_ref[pl.ds(pl.multiple_of(i * deep, group), deep), :] for i in near]
-            total = lax.dot_general(
-                cube_ref[slot + k],
-                jnp.concatenate(weights, axis=1),
-                (((1,), (1,)), ((), ())),
-                preferred_element_type=f32,
-            ).T
-            total = total[:group] + total[group : 2 * group] + total[2 * group :]
-            sums_ref[pl.ds(leaf, group, stride=leaves), :] = total
-
-    def both(step, carry):
-        sums(step - 1)
-        cubes(step)
-        return carry
-
-    steps = leaves // batch
-    cubes(0)
-    lax.fori_loop(1, steps, both, 0)
-    sums(steps - 1)
-
-    got = [sums_ref[pl.ds(row * leaves, leaves), :] for row in range(15)]
-    first, mixed, rest = got[:3], [got[3 + 3 * i : 6 + 3 * i] for i in range(3)], got[12:]
-    factor = live_ref[...] * inv_eight_pi
-    shift = dot3(own_place, first) - (mixed[0][0] + mixed[1][1] + mixed[2][2])
+    for k in range(count):
+        wide = target_wide_ref[(first + k) * height : (first + k + 1) * height, :]
+        target_ref[k * per_leaf : (k + 1) * per_leaf, :] = wide.T.astype(bf16)
+    for k in range(count):
+        target = target_ref[k * per_leaf : (k + 1) * per_leaf, :]
+        for n in range(0, nbr_count, 2):
+            near = [neighbours_ref[0, n + i, first + k] for i in range(2)]
+            points = [source_ref[pl.ds(pl.multiple_of(i * group, group), group), :] for i in near]
+            points = jnp.concatenate(points, axis=1)
+            dist_sq = jnp.dot(
+                target, jnp.concatenate([points, points], axis=0), preferred_element_type=f32
+            )
+            inverse = lax.rsqrt(dist_sq)
+            cube = (inverse * inverse * inverse).astype(bf16)
+            cube_ref[k, :, n * per_leaf : (n + 2) * per_leaf] = cube
+    for k in range(count):
+        near = [neighbours_ref[0, n, first + k] for n in range(nbr_count)]
+        weights = [weight_ref[pl.ds(pl.multiple_of(i * deep, group), deep), :] for i in near]
+        total = lax.dot_general(
+            cube_ref[k],
+            jnp.concatenate(weights, axis=1),
+            (((1,), (1,)), ((), ())),
+            preferred_element_type=f32,
+        ).T
+        total = total[:group] + total[group : 2 * group] + total[2 * group :]
+        sums_ref[pl.ds(k, group, stride=count), :] = total
+
+    got = [sums_ref[row * count : (row + 1) * count, :] for row in range(15)]
+    start, mixed, rest = got[:3], [got[3 + 3 * i : 6 + 3 * i] for i in range(3)], got[12:]
+    place = [sum(split(own_ref[axis, first : first + count, :], 2)) for axis in range(3)]
+    norm = dot3(place, place)
+    factor = live * inv_eight_pi
+    shift = dot3(place, start) - (mixed[0][0] + mixed[1][1] + mixed[2][2])
     for i in range(3):
-        turned = dot3(own_place, [2.0 * mixed[i][j] + mixed[j][i] for j in range(3)])
-        out_ref[i] = (own_norm * first[i] + own_place[i] * shift - turned + rest[i]) * factor
+        turned = dot3(place, [2.0 * mixed[i][j] + mixed[j][i] for j in range(3)])
+        out_ref[i] = (norm * start[i] + place[i] * shift - turned + rest[i]) * factor
 
 
 def far_field(sources_ref, rows_ref, tile_of, out_ref, out_hbm, pick_ref, moved_ref, out_sem):
@@ -233,10 +217,13 @@
     rows = rows_ref[:, :coeffs]
     stores = []
     for i, start in enumerate(range(0, coeffs, tile)):
-        ops_ref = tile_of(i)
+        parts = tile_of(i)
         size = min(tile, coeffs - start)
         for t in range(directions):
-            moved = jnp.dot(rows, ops_ref[t], preferred_element_type=f32)
+            deep = parts[0].shape[1]
+            moved = jnp.dot(rows[:, :deep], parts[0][t], preferred_element_type=f32)
+            if deep < coeffs:
+                moved += jnp.dot(rows[:, deep:], parts[1][t], preferred_element_type=f32)
             moved_ref[t * slot_count : (t + 1) * slot_count, :size] = moved.astype(bf16)
         for low in range(0, size, 2 * lanes):
             rest = min(2 * lanes, size - low)
@@ -256,37 +243,61 @@
 
 def near_kernel(
     slab_axis, neighbours_ref, live_ref, own_ref, odd_ref, even_ref, ops_hbm,
-    velocity_ref, head_ref,
-    point_ref, moment_ref, source_ref, weight_ref, target_wide_ref, target_ref, sums_ref, cube_ref, sem,
-):
-    head = pltpu.make_async_copy(ops_hbm.at[:, :, pl.ds(0, head_ref.shape[2])], head_ref, sem)
+    early_ref, head_ref,
+    point_ref, moment_ref, target_wide_ref, source_ref, weight_ref, target_ref, cube_ref, sums_ref, sem,
+):
+    at = (slice(None), pl.ds(0, head_ref.shape[1]), pl.ds(0, head_ref.shape[2]))
+    head = pltpu.make_async_copy(ops_hbm.at[at], head_ref, sem)
     head.start()
-    near_field(
-        slab_axis, neighbours_ref, live_ref, own_ref, even_ref, odd_ref, velocity_ref,
-        point_ref, moment_ref, source_ref, weight_ref, target_wide_ref, target_ref, sums_ref, cube_ref,
-    )
+    near_tables(
+        slab_axis, own_ref, even_ref, odd_ref,
+        point_ref, moment_ref, target_wide_ref, source_ref, weight_ref,
+    )
+    count = early_ref.shape[1]
+    near_leaves(
+        0, neighbours_ref, own_ref, live_ref[:count, :], target_wide_ref,
+        source_ref, weight_ref, target_ref, cube_ref, sums_ref, early_ref,
+    )
+    early_ref[3] = live_ref[count:, :]
     head.wait()
 
 
 def far_kernel(
-    picks_ref, rows_ref, head_ref, velocity_ref, ops_hbm, local_hbm, velocity_hbm,
-    ops_ref, pick_ref, moved_ref, local_ref, ops_sem, out_sem,
+    slab_axis, neighbours_ref, own_ref, odd_ref, even_ref, picks_ref, rows_ref, head_ref, early_ref,
+    ops_hbm, local_hbm, velocity_hbm,
+    point_ref, moment_ref, target_wide_ref, source_ref, weight_ref, target_ref, cube_ref, sums_ref,
+    ops_ref, pick_ref, moved_ref, local_ref, late_ref, velocity_ref, ops_sem, out_sem,
 ):
     coeffs, tile = ops_hbm.shape[1], moved_ref.shape[1]
-    loads = [None]
+    deep = head_ref.shape[1]
+    rest = (slice(None), pl.ds(deep, coeffs - deep), pl.ds(0, tile))
+    loads = [pltpu.make_async_copy(ops_hbm.at[rest], ops_ref.at[rest], ops_sem.at[0])]
+    loads[0].start()
     for i, start in enumerate(range(tile, coeffs, tile)):
         at = pl.ds(start, min(tile, coeffs - start))
-        loads.append(pltpu.make_async_copy(ops_hbm.at[:, :, at], ops_ref.at[:, :, at], ops_sem.at[i]))
+        loads.append(pltpu.make_async_copy(ops_hbm.at[:, :, at], ops_ref.at[:, :, at], ops_sem.at[i + 1]))
         loads[-1].start()
 
-    velocity_store = pltpu.make_async_copy(velocity_ref, velocity_hbm, ops_sem.at[len(loads) - 1])
+    count = early_ref.shape[1]
+    near_tables(
+        slab_axis, own_ref, even_ref, odd_ref,
+        point_ref, moment_ref, target_wide_ref, source_ref, weight_ref,
+    )
+    near_leaves(
+        count, neighbours_ref, own_ref, early_ref[3], target_wide_ref,
+        source_ref, weight_ref, target_ref, cube_ref, sums_ref, late_ref,
+    )
+    for axis in range(3):
+        velocity_ref[axis, :count, :] = early_ref[axis]
+        velocity_ref[axis, count:, :] = late_ref[axis]
+    velocity_store = pltpu.make_async_copy(velocity_ref, velocity_hbm, ops_sem.at[len(loads)])
     velocity_store.start()
 
     def tile_of(i):
+        loads[i].wait()
         if i == 0:
-            return head_ref
-        loads[i].wait()
-        return ops_ref.at[:, :, pl.ds(i * tile, min(tile, coeffs - i * tile))]
+            return (head_ref, ops_ref.at[rest])
+        return (ops_ref.at[:, :, pl.ds(i * tile, min(tile, coeffs - i * tile))],)
 
     stores = far_field(picks_ref, rows_ref, tile_of, local_ref, local_hbm, pick_ref, moved_ref, out_sem)
     for store in stores + [velocity_store]:
@@ -309,57 +320,67 @@
     return pl.BlockSpec(memory_space=pltpu.HBM)
 
 
+def near_scratch(neighbours, packed):
+    _, leaves, per_leaf = packed.shape
+    table, count = 3 * leaves, leaves // 2
+    return [
+        pltpu.VMEM((table * group, per_leaf), f32),
+        pltpu.VMEM((table * group, per_leaf), f32),
+        pltpu.VMEM((leaves * 2 * group, per_leaf), f32),
+        pltpu.VMEM((table * group, per_leaf), bf16),
+        pltpu.VMEM((table * pieces * group, per_leaf), bf16),
+        pltpu.VMEM((count * per_leaf, 2 * group), bf16),
+        pltpu.VMEM((count, per_leaf, neighbours.shape[1] * per_leaf), bf16),
+        pltpu.VMEM((group * count, per_leaf), f32),
+    ]
+
+
 def call_near(neighbours, live, packed, odd, even, m2l_ops, tile):
     _, leaves, per_leaf = packed.shape
     directions, coeffs, _ = m2l_ops.shape
-    table = 3 * leaves
     return pl.pallas_call(
         functools.partial(near_kernel, "nb"),
         out_shape=(
-            pltpu.VMEM((3, leaves, per_leaf), f32),
-            pltpu.VMEM((directions, coeffs, tile), bf16),
+            pltpu.VMEM((4, leaves // 2, per_leaf), f32),
+            pltpu.VMEM((directions, coeffs // lanes * lanes, tile), bf16),
         ),
         in_specs=[smem()] + [vmem()] * 4 + [hbm()],
         out_specs=(vmem(), vmem()),
-        scratch_shapes=[
-            pltpu.VMEM((table * 16, per_leaf), f32),
-            pltpu.VMEM((table * 16, per_leaf), f32),
-            pltpu.VMEM((table * 16, per_leaf), bf16),
-            pltpu.VMEM((table * 48, per_leaf), bf16),
-            pltpu.VMEM((leaves * 32, per_leaf), f32),
-            pltpu.VMEM((leaves * per_leaf, 32), bf16),
-            pltpu.VMEM((16 * leaves, per_leaf), f32),
-            pltpu.VMEM((2 * 8, per_leaf, neighbours.shape[1] * per_leaf), bf16),
-            pltpu.SemaphoreType.DMA,
-        ],
+        scratch_shapes=near_scratch(neighbours, packed) + [pltpu.SemaphoreType.DMA],
         compiler_params=pltpu.CompilerParams(vmem_limit_bytes=24 * 2**20),
         name="near",
     )(neighbours, live, packed, odd, even, in_hbm(m2l_ops))
 
 
-def call_far(m2l_sources, arrived, head, velocity, m2l_ops):
-    directions, coeffs, tile = head.shape
+def call_far(neighbours, packed, odd, even, m2l_sources, arrived, head, early, m2l_ops):
+    _, leaves, per_leaf = packed.shape
+    directions, coeffs, _ = m2l_ops.shape
+    tile = head.shape[2]
     owned = m2l_sources.shape[2]
     picks = directions * arrived.shape[0]
+    steps = -(-coeffs // tile)
     return pl.pallas_call(
-        far_kernel,
+        functools.partial(far_kernel, "nb"),
         out_shape=(
             jax.ShapeDtypeStruct((coeffs, owned), bf16),
-            jax.ShapeDtypeStruct(velocity.shape, f32),
+            jax.ShapeDtypeStruct((3, leaves, per_leaf), f32),
         ),
-        in_specs=[vmem()] * 4 + [hbm()],
+        in_specs=[smem()] + [vmem()] * 7 + [hbm()],
         out_specs=(hbm(), hbm()),
-        scratch_shapes=[
+        scratch_shapes=near_scratch(neighbours, packed)
+        + [
             pltpu.VMEM(m2l_ops.shape, bf16),
             pltpu.VMEM((picks, owned), bf16),
             pltpu.VMEM((picks, tile), bf16),
             pltpu.VMEM((coeffs, owned), bf16),
-            pltpu.SemaphoreType.DMA((-(-coeffs // tile),)),
-            pltpu.SemaphoreType.DMA((-(-coeffs // (2 * lanes)),)),
+            pltpu.VMEM((3, leaves - leaves // 2, per_leaf), f32),
+            pltpu.VMEM((3, leaves, per_leaf), f32),
+            pltpu.SemaphoreType.DMA((steps + 1,)),
+            pltpu.SemaphoreType.DMA((2 * steps,)),
         ],
         compiler_params=pltpu.CompilerParams(vmem_limit_bytes=40 * 2**20),
         name="far",
-    )(m2l_sources, arrived, head, velocity, in_hbm(m2l_ops))
+    )(neighbours, packed, odd, even, m2l_sources, arrived, head, early, in_hbm(m2l_ops))
 
 
 def call_presum(hx_count, partial_multipoles, shared_slots, positions, forces, leaf_counts, neighbours):
@@ -434,8 +455,10 @@
         sums.reshape(hx_count, -1, sums.shape[1]), "hx", split_axis=0, concat_axis=0, tiled=True
     ).reshape(sums.shape)
 
-    velocity, head = call_near(sources, live, packed, odd, even, m2l_ops, 4 * lanes)
-    local, velocity = call_far(m2l_sources, arrived, head, velocity, m2l_ops)
+    early, head = call_near(sources, live, packed, odd, even, m2l_ops, 4 * lanes)
+    local, velocity = call_far(
+        sources, packed, odd, even, m2l_sources, arrived, head, early, m2l_ops
+    )
 
     return local.T[None], velocity.reshape(positions.shape)
 

time: 24 us -> 23.5 us (0.979)
  Pallas kernels: 11.3 us -> 10.8 us
    pallas_call x1, Pallas kernels: 3.35 us -> 1.94 us  [call_near(): pl.pallas_call(functools.partial(near_kernel, 'nb'), out_shape=(pltpu.VME...]
    pallas_call x1, Pallas kernels: 5.07 us -> 5.94 us  [call_far(): pl.pallas_call(functools.partial(far_kernel, 'nb'), out_shape=(jax.ShapeD...]
  transfers between devices with their start and end apart: 3 -> 3, of which waited for: 2 -> 2; matrix products, arithmetic and copies ran while one was open for 0% -> 0% of each run, Pallas kernels for 14% -> 8%
where the time goes in v4:
time: 23.5 us; the launch traced here: 23.2 us
  Pallas kernels  10.8 us (46%)
  starting transfers between devices  7.75 us (33%)
  waiting for transfers between devices  4.06 us (17%)
  between operations  0.67 us (3%)
    pallas_call x1, Pallas kernels, call_far(): pl.pallas_call(functools.partial(far_kernel, 'nb'), out_shape=(jax.ShapeD...  5.94 us
    all_to_all x1, starting transfers between devices, on_device(): lax.all_to_all(sums.reshape(hx_count, -1, sums.shape[1]), 'hx', split_axi...  4.26 us
    ppermute x1, waiting for transfers between devices, on_device(): odd = lax.ppermute(packed, 'nb', odd_pairs + [(j, i) for i, j in odd_pairs])  3.46 us
    pallas_call x1, Pallas kernels, call_presum(): pl.pallas_call(functools.partial(presum_kernel, cap, uniq, tile), out_sha...  2.88 us
    pallas_call x1, Pallas kernels, call_near(): pl.pallas_call(functools.partial(near_kernel, 'nb'), out_shape=(pltpu.VME...  1.94 us
    ppermute x1, starting transfers between devices, on_device(): odd = lax.ppermute(packed, 'nb', odd_pairs + [(j, i) for i, j in odd_pairs])  1.91 us
    ppermute x1, starting transfers between devices, on_device(): lax.ppermute(packed, 'nb', even_pairs + [(j, i) for i, j in even_pairs])  1.58 us
    ppermute x1, waiting for transfers between devices, on_device(): lax.ppermute(packed, 'nb', even_pairs + [(j, i) for i, j in even_pairs])  0.59 us
  transfers between devices with their start and end apart: 3, of which 2 were waited for; matrix products, arithmetic and copies ran while one was open for 0% of the time, Pallas kernels for 8%

profile of v4, /device:TPU:18, one launch (start us, length us, event | category | flops | bytes accessed | tf_op | source)
XLA Modules:
  0.0 23.2 jit_solution(4554823568702474451)
XLA Ops:
  0.6 2.9 %presum.1 = (bf16[128,1536]{1,0:T(8,128)(2,1)}, f32[6,16,128]{2,1,0:T(8,128)S(1)}, f32[16,128]{1,0:T(8,128)S(1)}, s32[1,8,16]{2,1,0:T(8,128)S(4)}) custom-call(s32[1,16]{1,0:T(1,128)} %counts_hbm.1, s32[1,512]{1,0:T(1,128)} %slots_hbm.1, bf16[1464,512]{1,0:T(8,128)(2,1)} %bitcast.12, f32[3,16,128]{2,1,0:T(8,128)} %bitcast.13, f32[3,16,128]{2,1,0:T(8,128)} %bitcast.14, ...), custom_call_target="tpu_custom_call" | custom-call | tf_op jit(solution)/shard_map/presum/pallas_call | solution.py:397
  3.5 4.3 %all-to-all-start = ((bf16[8,16,1536]{2,1,0:T(8,128)(2,1)}), bf16[8,16,1536]{2,1,0:T(8,128)(2,1)S(1)}, u32[]{:S(2)}, u32[]{:S(2)}) async-start(bf16[8,16,1536]{2,1,0:T(8,128)(2,1)} %bitcast.4), calls=%async_computation | async-start | bytes 786432 | tf_op jit(solution)/shard_map/all_to_all | solution.py:454
  7.8 1.6 %collective-permute-start.1 = (f32[6,16,128]{2,1,0:T(8,128)S(1)}, f32[6,16,128]{2,1,0:T(8,128)S(1)}, u32[]{:S(2)}, u32[]{:S(2)}) collective-permute-start(f32[6,16,128]{2,1,0:T(8,128)S(1)} %get-tuple-element.11.own_ref), channel_id=1, source_target_pairs={{0,1},{2,3},{1,0},{3,2},{4,5},{6,7},{5,4},{7,6},{8,9},{10,11},{9,8... | collective-permute-start | bytes 147464 | tf_op jit(solution)/shard_map/ppermute | solution.py:452
  9.4 1.9 %collective-permute-start = (f32[6,16,128]{2,1,0:T(8,128)S(1)}, f32[6,16,128]{2,1,0:T(8,128)S(1)}, u32[]{:S(2)}, u32[]{:S(2)}) collective-permute-start(f32[6,16,128]{2,1,0:T(8,128)S(1)} %get-tuple-element.11.own_ref), channel_id=1, source_target_pairs={{1,2},{2,1},{5,6},{6,5},{9,10},{10,9},{13,14},{14,13},{17,18},{18,... | collective-permute-start | bytes 147464 | tf_op jit(solution)/shard_map/ppermute | solution.py:453
  11.3 0.6 %collective-permute-done.1.even_ref = f32[6,16,128]{2,1,0:T(8,128)S(1)} collective-permute-done((f32[6,16,128]{2,1,0:T(8,128)S(1)}, f32[6,16,128]{2,1,0:T(8,128)S(1)}, u32[]{:S(2)}, u32[]{:S(2)}) %collective-permute-start.1) | collective-permute-done | bytes 49184 | tf_op jit(solution)/shard_map/ppermute | solution.py:452
  11.9 3.5 %collective-permute-done.odd_ref = f32[6,16,128]{2,1,0:T(8,128)S(1)} collective-permute-done((f32[6,16,128]{2,1,0:T(8,128)S(1)}, f32[6,16,128]{2,1,0:T(8,128)S(1)}, u32[]{:S(2)}, u32[]{:S(2)}) %collective-permute-start) | collective-permute-done | bytes 49184 | tf_op jit(solution)/shard_map/ppermute | solution.py:453
  15.3 0.0 copy-start
  15.3 1.9 %near.1 = (f32[4,8,128]{2,1,0:T(8,128)S(1)}, bf16[2,1408,512]{2,1,0:T(8,128)(2,1)S(1)}) custom-call(s32[1,8,16]{2,1,0:T(8,128)S(4)} %get-tuple-element.10.neighbours_ref, f32[16,128]{1,0:T(8,128)S(1)} %get-tuple-element.13.live_ref, f32[6,16,128]{2,1,0:T(8,128)S(1)} %get-tuple-element.11.own_ref, f32[6,16,128]{2,1,0:T(8,128)S(1)} %collective-permute-done.odd_ref, ...), custom_call_target="tpu_custom_call" | custom-call | tf_op jit(solution)/shard_map/near/pallas_call | solution.py:341
  17.3 0.0 all-to-all-done
  17.3 0.0 copy-done
  17.3 5.9 %far.1 = (bf16[1464,1024]{1,0:T(8,128)(2,1)}, f32[3,16,128]{2,1,0:T(8,128)}) custom-call(s32[1,8,16]{2,1,0:T(8,128)S(4)} %get-tuple-element.10.neighbours_ref, f32[6,16,128]{2,1,0:T(8,128)S(1)} %get-tuple-element.11.own_ref, f32[6,16,128]{2,1,0:T(8,128)S(1)} %collective-permute-done.odd_ref, f32[6,16,128]{2,1,0:T(8,128)S(1)} %collective-permute-done.1.even_ref, ...), custom_call_target="tpu_custom_call" | custom-call | tf_op jit(solution)/shard_map/far/pallas_call | solution.py:362
Async XLA Ops:
  3.5 13.8 %all-to-all-start = ((bf16[8,16,1536]{2,1,0:T(8,128)(2,1)}), bf16[8,16,1536]{2,1,0:T(8,128)(2,1)S(1)}, u32[]{:S(2)}, u32[]{:S(2)}) async-start(bf16[8,16,1536]{2,1,0:T(8,128)(2,1)} %bitcast.4), calls=%async_computation | async-start | bytes 786432 | tf_op jit(solution)/shard_map/all_to_all | solution.py:454
  7.8 4.1 %collective-permute-start.1 = (f32[6,16,128]{2,1,0:T(8,128)S(1)}, f32[6,16,128]{2,1,0:T(8,128)S(1)}, u32[]{:S(2)}, u32[]{:S(2)}) collective-permute-start(f32[6,16,128]{2,1,0:T(8,128)S(1)} %get-tuple-element.11.own_ref), channel_id=1, source_target_pairs={{0,1},{2,3},{1,0},{3,2},{4,5},{6,7},{5,4},{7,6},{8,9},{10,11},{9,8... | collective-permute-start | bytes 147464 | tf_op jit(solution)/shard_map/ppermute | solution.py:452
  9.4 6.0 %collective-permute-start = (f32[6,16,128]{2,1,0:T(8,128)S(1)}, f32[6,16,128]{2,1,0:T(8,128)S(1)}, u32[]{:S(2)}, u32[]{:S(2)}) collective-permute-start(f32[6,16,128]{2,1,0:T(8,128)S(1)} %get-tuple-element.11.own_ref), channel_id=1, source_target_pairs={{1,2},{2,1},{5,6},{6,5},{9,10},{10,9},{13,14},{14,13},{17,18},{18,... | collective-permute-start | bytes 147464 | tf_op jit(solution)/shard_map/ppermute | solution.py:453
  15.3 2.0 %copy-start = (s32[1,2,1024]{2,1,0:T(2,128)S(1)}, s32[1,2,1024]{2,1,0:T(2,128)}, u32[]{:S(2)}) copy-start(s32[1,2,1024]{2,1,0:T(2,128)} %picks_ref.1) | copy-start | bytes 24580

commit v5 on v4

--- a/solution.py
+++ b/solution.py
@@ -29,7 +29,7 @@
 
 def presum_kernel(
     cap, uniq, tile, counts_hbm, slots_hbm, rows_hbm, pos_hbm, frc_hbm, neighbours_hbm,
-    sums_hbm, packed_ref, live_ref, neighbours_out,
+    sums_hbm, packed_ref, sent_ref, live_ref, neighbours_out,
     counts_ref, slots_ref, rows_ref, pos_ref, frc_ref, sums_ref, arrival, rows_sem, sums_sem,
 ):
     coeffs, row_count = rows_ref.shape
@@ -100,8 +100,12 @@
     live = jnp.where(point_at < count, 1.0, 0.0)
     live_ref[...] = live
     for axis in range(3):
+        masked = frc_ref[axis] * live
         packed_ref[axis] = pos_ref[axis]
-        packed_ref[3 + axis] = frc_ref[axis] * live
+        packed_ref[3 + axis] = masked
+        high, low = split(pos_ref[axis], 2)
+        for row, value in enumerate((high, low, masked)):
+            sent_ref[3 * row + axis] = value.astype(bf16)
     for store in stores:
         store.wait()
 
@@ -121,15 +125,15 @@
             ref[pl.ds(leaf_start * height + row, leaves, stride=height), :] = value
 
     for part in range(3):
-        if part == 0:
-            comp = [jnp.where(even, odd_ref[c], even_ref[c]) for c in range(6)]
-        elif part == 1:
-            comp = [own_ref[c] for c in range(6)]
+        if part == 1:
+            cut = [split(own_ref[c], 2) for c in range(3)]
+            force = [own_ref[3 + c] for c in range(3)]
         else:
-            comp = [jnp.where(even, even_ref[c], odd_ref[c]) for c in range(6)]
-        cut = [split(c, 2) for c in comp[:3]]
+            refs = (odd_ref, even_ref) if part == 0 else (even_ref, odd_ref)
+            comp = [jnp.where(even, refs[0][c], refs[1][c]).astype(f32) for c in range(9)]
+            cut = [comp[c : c + 4 : 3] for c in range(3)]
+            force = comp[6:]
         place = [high + low for high, low in cut]
-        force = comp[3:]
         norm = dot3(place, place)
         along = dot3(force, place)
         size = split(norm + reg_eps2, 3)
@@ -399,11 +403,12 @@
         out_shape=(
             jax.ShapeDtypeStruct((slot_count, width), bf16),
             pltpu.VMEM((6, leaves, per_leaf), f32),
+            pltpu.VMEM((9, leaves, per_leaf), bf16),
             pltpu.VMEM((leaves, per_leaf), f32),
             pltpu.SMEM(neighbours.shape, jnp.int32),
         ),
         in_specs=[hbm()] * 6,
-        out_specs=(hbm(), vmem(), vmem(), smem()),
+        out_specs=(hbm(), vmem(), vmem(), vmem(), smem()),
         scratch_shapes=[
             pltpu.VMEM(leaf_counts.shape, jnp.int32),
             pltpu.VMEM(shared_slots.shape, jnp.int32),
@@ -443,14 +448,14 @@
     neighbours,
 ):
     hx_count, nb_count = lax.axis_size("hx"), lax.axis_size("nb")
-    sums, packed, live, sources = call_presum(
+    sums, packed, sent, live, sources = call_presum(
         hx_count, partial_multipoles, shared_slots, positions, forces, leaf_counts, neighbours
     )
 
     even_pairs = [(i, i + 1) for i in range(0, nb_count - 1, 2)]
     odd_pairs = [(i, i + 1) for i in range(1, nb_count - 1, 2)]
-    even = lax.ppermute(packed, "nb", even_pairs + [(j, i) for i, j in even_pairs])
-    odd = lax.ppermute(packed, "nb", odd_pairs + [(j, i) for i, j in odd_pairs])
+    even = lax.ppermute(sent, "nb", even_pairs + [(j, i) for i, j in even_pairs])
+    odd = lax.ppermute(sent, "nb", odd_pairs + [(j, i) for i, j in odd_pairs])
     arrived = lax.all_to_all(
         sums.reshape(hx_count, -1, sums.shape[1]), "hx", split_axis=0, concat_axis=0, tiled=True
     ).reshape(sums.shape)

time: 23.5 us -> 23.4 us (level)
  the two profiles are of different devices: /device:TPU:18 before, /device:TPU:0 now
where the time goes in v5:
time: 23.4 us; the launch traced here: 23 us
  Pallas kernels  10.8 us (46%)
  starting transfers between devices  7.41 us (32%)
  waiting for transfers between devices  4.16 us (18%)
  between operations  0.66 us (3%)
    pallas_call x1, Pallas kernels, call_far(): pl.pallas_call(functools.partial(far_kernel, 'nb'), out_shape=(jax.ShapeD...  5.94 us
    all_to_all x1, starting transfers between devices, on_device(): lax.all_to_all(sums.reshape(hx_count, -1, sums.shape[1]), 'hx', split_axi...  5.18 us
    pallas_call x1, Pallas kernels, call_presum(): pl.pallas_call(functools.partial(presum_kernel, cap, uniq, tile), out_sha...  2.88 us
    all_to_all x1, waiting for transfers between devices, on_device(): lax.all_to_all(sums.reshape(hx_count, -1, sums.shape[1]), 'hx', split_axi...  2.44 us
    pallas_call x1, Pallas kernels, call_near(): pl.pallas_call(functools.partial(near_kernel, 'nb'), out_shape=(pltpu.VME...  1.93 us
    ppermute x1, waiting for transfers between devices, on_device(): lax.ppermute(sent, 'nb', even_pairs + [(j, i) for i, j in even_pairs])  1.72 us
    ppermute x1, starting transfers between devices, on_device(): lax.ppermute(sent, 'nb', even_pairs + [(j, i) for i, j in even_pairs])  1.58 us
    ppermute x1, starting transfers between devices, on_device(): odd = lax.ppermute(sent, 'nb', odd_pairs + [(j, i) for i, j in odd_pairs])  0.65 us
  transfers between devices with their start and end apart: 3, of which 2 were waited for; matrix products, arithmetic and copies ran while one was open for 0% of the time, Pallas kernels for 8%

profile of v5, /device:TPU:0, one launch (start us, length us, event | category | flops | bytes accessed | tf_op | source)
XLA Modules:
  0.0 23.0 jit_solution(13078984957649808014)
XLA Ops:
  0.6 2.9 %presum.1 = (bf16[128,1536]{1,0:T(8,128)(2,1)}, f32[6,16,128]{2,1,0:T(8,128)S(1)}, bf16[9,16,128]{2,1,0:T(8,128)(2,1)S(1)}, f32[16,128]{1,0:T(8,128)S(1)}, s32[1,8,16]{2,1,0:T(8,128)S(4)}) custom-call(s32[1,16]{1,0:T(1,128)} %counts_hbm.1, s32[1,512]{1,0:T(1,128)} %slots_hbm.1, bf16[1464,512]{1,0:T(8,128)(2,1)} %bitcast.12, f32[3,16,128]{2,1,0:T(8,128)} %bitcast.13, ...), custom_call_target="tpu_custom_call" | custom-call | tf_op jit(solution)/shard_map/presum/pallas_call | solution.py:401
  3.5 5.2 %all-to-all-start = ((bf16[8,16,1536]{2,1,0:T(8,128)(2,1)}), bf16[8,16,1536]{2,1,0:T(8,128)(2,1)S(1)}, u32[]{:S(2)}, u32[]{:S(2)}) async-start(bf16[8,16,1536]{2,1,0:T(8,128)(2,1)} %bitcast.4), calls=%async_computation | async-start | bytes 786432 | tf_op jit(solution)/shard_map/all_to_all | solution.py:459
  8.7 1.6 %collective-permute-start.1 = (bf16[9,16,128]{2,1,0:T(8,128)(2,1)S(1)}, bf16[9,16,128]{2,1,0:T(8,128)(2,1)S(1)}, u32[]{:S(2)}, u32[]{:S(2)}) collective-permute-start(bf16[9,16,128]{2,1,0:T(8,128)(2,1)S(1)} %get-tuple-element.13), channel_id=1, source_target_pairs={{0,1},{2,3},{1,0},{3,2},{4,5},{6,7},{5,4},{7,6},{8,9},{10,11},{9,8... | collective-permute-start | bytes 110600 | tf_op jit(solution)/shard_map/ppermute | solution.py:457
  10.3 0.7 %collective-permute-start = (bf16[9,16,128]{2,1,0:T(8,128)(2,1)S(1)}, bf16[9,16,128]{2,1,0:T(8,128)(2,1)S(1)}, u32[]{:S(2)}, u32[]{:S(2)}) collective-permute-start(bf16[9,16,128]{2,1,0:T(8,128)(2,1)S(1)} %get-tuple-element.13), channel_id=1, source_target_pairs={{1,2},{2,1},{5,6},{6,5},{9,10},{10,9},{13,14},{14,13},{17,18},{18,... | collective-permute-start | bytes 110600 | tf_op jit(solution)/shard_map/ppermute | solution.py:458
  10.9 1.7 %collective-permute-done.1.even_ref = bf16[9,16,128]{2,1,0:T(8,128)(2,1)S(1)} collective-permute-done((bf16[9,16,128]{2,1,0:T(8,128)(2,1)S(1)}, bf16[9,16,128]{2,1,0:T(8,128)(2,1)S(1)}, u32[]{:S(2)}, u32[]{:S(2)}) %collective-permute-start.1) | collective-permute-done | bytes 36896 | tf_op jit(solution)/shard_map/ppermute | solution.py:457
  12.7 0.0 collective-permute-done.odd_ref
  12.7 0.0 copy-start
  12.7 1.9 %near.1 = (f32[4,8,128]{2,1,0:T(8,128)S(1)}, bf16[2,1408,512]{2,1,0:T(8,128)(2,1)S(1)}) custom-call(s32[1,8,16]{2,1,0:T(8,128)S(4)} %get-tuple-element.11.neighbours_ref, f32[16,128]{1,0:T(8,128)S(1)} %get-tuple-element.15.live_ref, f32[6,16,128]{2,1,0:T(8,128)S(1)} %get-tuple-element.12.own_ref, bf16[9,16,128]{2,1,0:T(8,128)(2,1)S(1)} %collective-permute-done.odd_ref, ...), custom_call_target="tpu_custom_call" | custom-call | tf_op jit(solution)/shard_map/near/pallas_call | solution.py:345
  14.6 2.4 %all-to-all-done = bf16[8,16,1536]{2,1,0:T(8,128)(2,1)S(1)} async-done(((bf16[8,16,1536]{2,1,0:T(8,128)(2,1)}), bf16[8,16,1536]{2,1,0:T(8,128)(2,1)S(1)}, u32[]{:S(2)}, u32[]{:S(2)}) %all-to-all-start) | async-done | bytes 393248 | tf_op jit(solution)/shard_map/all_to_all | solution.py:459
  17.0 0.0 copy-done
  17.0 5.9 %far.1 = (bf16[1464,1024]{1,0:T(8,128)(2,1)}, f32[3,16,128]{2,1,0:T(8,128)}) custom-call(s32[1,8,16]{2,1,0:T(8,128)S(4)} %get-tuple-element.11.neighbours_ref, f32[6,16,128]{2,1,0:T(8,128)S(1)} %get-tuple-element.12.own_ref, bf16[9,16,128]{2,1,0:T(8,128)(2,1)S(1)} %collective-permute-done.odd_ref, bf16[9,16,128]{2,1,0:T(8,128)(2,1)S(1)} %collective-permute-done.1.even_ref, ...), custom_call_target="tpu_custom_call" | custom-call | tf_op jit(solution)/shard_map/far/pallas_call | solution.py:366
Async XLA Ops:
  3.5 13.5 %all-to-all-start = ((bf16[8,16,1536]{2,1,0:T(8,128)(2,1)}), bf16[8,16,1536]{2,1,0:T(8,128)(2,1)S(1)}, u32[]{:S(2)}, u32[]{:S(2)}) async-start(bf16[8,16,1536]{2,1,0:T(8,128)(2,1)} %bitcast.4), calls=%async_computation | async-start | bytes 786432 | tf_op jit(solution)/shard_map/all_to_all | solution.py:459
  8.7 4.0 %collective-permute-start.1 = (bf16[9,16,128]{2,1,0:T(8,128)(2,1)S(1)}, bf16[9,16,128]{2,1,0:T(8,128)(2,1)S(1)}, u32[]{:S(2)}, u32[]{:S(2)}) collective-permute-start(bf16[9,16,128]{2,1,0:T(8,128)(2,1)S(1)} %get-tuple-element.13), channel_id=1, source_target_pairs={{0,1},{2,3},{1,0},{3,2},{4,5},{6,7},{5,4},{7,6},{8,9},{10,11},{9,8... | collective-permute-start | bytes 110600 | tf_op jit(solution)/shard_map/ppermute | solution.py:457
  10.3 2.4 %collective-permute-start = (bf16[9,16,128]{2,1,0:T(8,128)(2,1)S(1)}, bf16[9,16,128]{2,1,0:T(8,128)(2,1)S(1)}, u32[]{:S(2)}, u32[]{:S(2)}) collective-permute-start(bf16[9,16,128]{2,1,0:T(8,128)(2,1)S(1)} %get-tuple-element.13), channel_id=1, source_target_pairs={{1,2},{2,1},{5,6},{6,5},{9,10},{10,9},{13,14},{14,13},{17,18},{18,... | collective-permute-start | bytes 110600 | tf_op jit(solution)/shard_map/ppermute | solution.py:458
  12.7 4.4 %copy-start = (s32[1,2,1024]{2,1,0:T(2,128)S(1)}, s32[1,2,1024]{2,1,0:T(2,128)}, u32[]{:S(2)}) copy-start(s32[1,2,1024]{2,1,0:T(2,128)} %picks_ref.1) | copy-start | bytes 24580

commit v6 on v5

--- a/solution.py
+++ b/solution.py
@@ -221,13 +221,10 @@
     rows = rows_ref[:, :coeffs]
     stores = []
     for i, start in enumerate(range(0, coeffs, tile)):
-        parts = tile_of(i)
+        ops_ref = tile_of(i)
         size = min(tile, coeffs - start)
         for t in range(directions):
-            deep = parts[0].shape[1]
-            moved = jnp.dot(rows[:, :deep], parts[0][t], preferred_element_type=f32)
-            if deep < coeffs:
-                moved += jnp.dot(rows[:, deep:], parts[1][t], preferred_element_type=f32)
+            moved = jnp.dot(rows, ops_ref[t], preferred_element_type=f32)
             moved_ref[t * slot_count : (t + 1) * slot_count, :size] = moved.astype(bf16)
         for low in range(0, size, 2 * lanes):
             rest = min(2 * lanes, size - low)
@@ -273,10 +270,7 @@
     ops_ref, pick_ref, moved_ref, local_ref, late_ref, velocity_ref, ops_sem, out_sem,
 ):
     coeffs, tile = ops_hbm.shape[1], moved_ref.shape[1]
-    deep = head_ref.shape[1]
-    rest = (slice(None), pl.ds(deep, coeffs - deep), pl.ds(0, tile))
-    loads = [pltpu.make_async_copy(ops_hbm.at[rest], ops_ref.at[rest], ops_sem.at[0])]
-    loads[0].start()
+    loads = [None]
     for i, start in enumerate(range(tile, coeffs, tile)):
         at = pl.ds(start, min(tile, coeffs - start))
         loads.append(pltpu.make_async_copy(ops_hbm.at[:, :, at], ops_ref.at[:, :, at], ops_sem.at[i + 1]))
@@ -298,10 +292,10 @@
     velocity_store.start()
 
     def tile_of(i):
+        if i == 0:
+            return head_ref
         loads[i].wait()
-        if i == 0:
-            return (head_ref, ops_ref.at[rest])
-        return (ops_ref.at[:, :, pl.ds(i * tile, min(tile, coeffs - i * tile))],)
+        return ops_ref.at[:, :, pl.ds(i * tile, min(tile, coeffs - i * tile))]
 
     stores = far_field(picks_ref, rows_ref, tile_of, local_ref, local_hbm, pick_ref, moved_ref, out_sem)
     for store in stores + [velocity_store]:
@@ -346,7 +340,7 @@
         functools.partial(near_kernel, "nb"),
         out_shape=(
             pltpu.VMEM((4, leaves // 2, per_leaf), f32),
-            pltpu.VMEM((directions, coeffs // lanes * lanes, tile), bf16),
+            pltpu.VMEM((directions, coeffs, tile), bf16),
         ),
         in_specs=[smem()] + [vmem()] * 4 + [hbm()],
         out_specs=(vmem(), vmem()),

time: 23.4 us -> 23.1 us (0.987)
  Pallas kernels: 10.8 us -> 10.4 us
    pallas_call x1, Pallas kernels: 5.94 us -> 5.63 us  [call_far(): pl.pallas_call(functools.partial(far_kernel, 'nb'), out_shape=(jax.ShapeD...]
where the time goes in v6:
time: 23.1 us; the launch traced here: 22.7 us
  Pallas kernels  10.4 us (45%)
  starting transfers between devices  7.41 us (32%)
  waiting for transfers between devices  4.17 us (18%)
  between operations  0.66 us (3%)
    pallas_call x1, Pallas kernels, call_far(): pl.pallas_call(functools.partial(far_kernel, 'nb'), out_shape=(jax.ShapeD...  5.63 us
    all_to_all x1, starting transfers between devices, on_device(): lax.all_to_all(sums.reshape(hx_count, -1, sums.shape[1]), 'hx', split_axi...  5.18 us
    pallas_call x1, Pallas kernels, call_presum(): pl.pallas_call(functools.partial(presum_kernel, cap, uniq, tile), out_sha...  2.88 us
    all_to_all x1, waiting for transfers between devices, on_device(): lax.all_to_all(sums.reshape(hx_count, -1, sums.shape[1]), 'hx', split_axi...  2.44 us
    pallas_call x1, Pallas kernels, call_near(): pl.pallas_call(functools.partial(near_kernel, 'nb'), out_shape=(pltpu.VME...  1.92 us
    ppermute x1, waiting for transfers between devices, on_device(): lax.ppermute(sent, 'nb', even_pairs + [(j, i) for i, j in even_pairs])  1.72 us
    ppermute x1, starting transfers between devices, on_device(): lax.ppermute(sent, 'nb', even_pairs + [(j, i) for i, j in even_pairs])  1.58 us
    ppermute x1, starting transfers between devices, on_device(): odd = lax.ppermute(sent, 'nb', odd_pairs + [(j, i) for i, j in odd_pairs])  0.65 us
  transfers between devices with their start and end apart: 3, of which 2 were waited for; matrix products, arithmetic and copies ran while one was open for 0% of the time, Pallas kernels for 8%

profile of v6, /device:TPU:0, one launch (start us, length us, event | category | flops | bytes accessed | tf_op | source)
XLA Modules:
  0.0 22.7 jit_solution(15160188443141876694)
XLA Ops:
  0.6 2.9 %presum.1 = (bf16[128,1536]{1,0:T(8,128)(2,1)}, f32[6,16,128]{2,1,0:T(8,128)S(1)}, bf16[9,16,128]{2,1,0:T(8,128)(2,1)S(1)}, f32[16,128]{1,0:T(8,128)S(1)}, s32[1,8,16]{2,1,0:T(8,128)S(4)}) custom-call(s32[1,16]{1,0:T(1,128)} %counts_hbm.1, s32[1,512]{1,0:T(1,128)} %slots_hbm.1, bf16[1464,512]{1,0:T(8,128)(2,1)} %bitcast.12, f32[3,16,128]{2,1,0:T(8,128)} %bitcast.13, ...), custom_call_target="tpu_custom_call" | custom-call | tf_op jit(solution)/shard_map/presum/pallas_call | solution.py:395
  3.5 5.2 %all-to-all-start = ((bf16[8,16,1536]{2,1,0:T(8,128)(2,1)}), bf16[8,16,1536]{2,1,0:T(8,128)(2,1)S(1)}, u32[]{:S(2)}, u32[]{:S(2)}) async-start(bf16[8,16,1536]{2,1,0:T(8,128)(2,1)} %bitcast.4), calls=%async_computation | async-start | bytes 786432 | tf_op jit(solution)/shard_map/all_to_all | solution.py:453
  8.7 1.6 %collective-permute-start.1 = (bf16[9,16,128]{2,1,0:T(8,128)(2,1)S(1)}, bf16[9,16,128]{2,1,0:T(8,128)(2,1)S(1)}, u32[]{:S(2)}, u32[]{:S(2)}) collective-permute-start(bf16[9,16,128]{2,1,0:T(8,128)(2,1)S(1)} %get-tuple-element.13), channel_id=1, source_target_pairs={{0,1},{2,3},{1,0},{3,2},{4,5},{6,7},{5,4},{7,6},{8,9},{10,11},{9,8... | collective-permute-start | bytes 110600 | tf_op jit(solution)/shard_map/ppermute | solution.py:451
  10.3 0.7 %collective-permute-start = (bf16[9,16,128]{2,1,0:T(8,128)(2,1)S(1)}, bf16[9,16,128]{2,1,0:T(8,128)(2,1)S(1)}, u32[]{:S(2)}, u32[]{:S(2)}) collective-permute-start(bf16[9,16,128]{2,1,0:T(8,128)(2,1)S(1)} %get-tuple-element.13), channel_id=1, source_target_pairs={{1,2},{2,1},{5,6},{6,5},{9,10},{10,9},{13,14},{14,13},{17,18},{18,... | collective-permute-start | bytes 110600 | tf_op jit(solution)/shard_map/ppermute | solution.py:452
  10.9 1.7 %collective-permute-done.1.even_ref = bf16[9,16,128]{2,1,0:T(8,128)(2,1)S(1)} collective-permute-done((bf16[9,16,128]{2,1,0:T(8,128)(2,1)S(1)}, bf16[9,16,128]{2,1,0:T(8,128)(2,1)S(1)}, u32[]{:S(2)}, u32[]{:S(2)}) %collective-permute-start.1) | collective-permute-done | bytes 36896 | tf_op jit(solution)/shard_map/ppermute | solution.py:451
  12.7 0.0 collective-permute-done.odd_ref
  12.7 0.0 copy-start
  12.7 1.9 %near.1 = (f32[4,8,128]{2,1,0:T(8,128)S(1)}, bf16[2,1464,512]{2,1,0:T(8,128)(2,1)S(1)}) custom-call(s32[1,8,16]{2,1,0:T(8,128)S(4)} %get-tuple-element.11.neighbours_ref, f32[16,128]{1,0:T(8,128)S(1)} %get-tuple-element.15.live_ref, f32[6,16,128]{2,1,0:T(8,128)S(1)} %get-tuple-element.12.own_ref, bf16[9,16,128]{2,1,0:T(8,128)(2,1)S(1)} %collective-permute-done.odd_ref, ...), custom_call_target="tpu_custom_call" | custom-call | tf_op jit(solution)/shard_map/near/pallas_call | solution.py:339
  14.6 2.4 %all-to-all-done = bf16[8,16,1536]{2,1,0:T(8,128)(2,1)S(1)} async-done(((bf16[8,16,1536]{2,1,0:T(8,128)(2,1)}), bf16[8,16,1536]{2,1,0:T(8,128)(2,1)S(1)}, u32[]{:S(2)}, u32[]{:S(2)}) %all-to-all-start) | async-done | bytes 393248 | tf_op jit(solution)/shard_map/all_to_all | solution.py:453
  17.0 0.0 copy-done
  17.0 5.6 %far.1 = (bf16[1464,1024]{1,0:T(8,128)(2,1)}, f32[3,16,128]{2,1,0:T(8,128)}) custom-call(s32[1,8,16]{2,1,0:T(8,128)S(4)} %get-tuple-element.11.neighbours_ref, f32[6,16,128]{2,1,0:T(8,128)S(1)} %get-tuple-element.12.own_ref, bf16[9,16,128]{2,1,0:T(8,128)(2,1)S(1)} %collective-permute-done.odd_ref, bf16[9,16,128]{2,1,0:T(8,128)(2,1)S(1)} %collective-permute-done.1.even_ref, ...), custom_call_target="tpu_custom_call" | custom-call | tf_op jit(solution)/shard_map/far/pallas_call | solution.py:360
Async XLA Ops:
  3.5 13.5 %all-to-all-start = ((bf16[8,16,1536]{2,1,0:T(8,128)(2,1)}), bf16[8,16,1536]{2,1,0:T(8,128)(2,1)S(1)}, u32[]{:S(2)}, u32[]{:S(2)}) async-start(bf16[8,16,1536]{2,1,0:T(8,128)(2,1)} %bitcast.4), calls=%async_computation | async-start | bytes 786432 | tf_op jit(solution)/shard_map/all_to_all | solution.py:453
  8.7 4.0 %collective-permute-start.1 = (bf16[9,16,128]{2,1,0:T(8,128)(2,1)S(1)}, bf16[9,16,128]{2,1,0:T(8,128)(2,1)S(1)}, u32[]{:S(2)}, u32[]{:S(2)}) collective-permute-start(bf16[9,16,128]{2,1,0:T(8,128)(2,1)S(1)} %get-tuple-element.13), channel_id=1, source_target_pairs={{0,1},{2,3},{1,0},{3,2},{4,5},{6,7},{5,4},{7,6},{8,9},{10,11},{9,8... | collective-permute-start | bytes 110600 | tf_op jit(solution)/shard_map/ppermute | solution.py:451
  10.3 2.4 %collective-permute-start = (bf16[9,16,128]{2,1,0:T(8,128)(2,1)S(1)}, bf16[9,16,128]{2,1,0:T(8,128)(2,1)S(1)}, u32[]{:S(2)}, u32[]{:S(2)}) collective-permute-start(bf16[9,16,128]{2,1,0:T(8,128)(2,1)S(1)} %get-tuple-element.13), channel_id=1, source_target_pairs={{1,2},{2,1},{5,6},{6,5},{9,10},{10,9},{13,14},{14,13},{17,18},{18,... | collective-permute-start | bytes 110600 | tf_op jit(solution)/shard_map/ppermute | solution.py:452
  12.7 4.4 %copy-start = (s32[1,2,1024]{2,1,0:T(2,128)S(1)}, s32[1,2,1024]{2,1,0:T(2,128)}, u32[]{:S(2)}) copy-start(s32[1,2,1024]{2,1,0:T(2,128)} %picks_ref.1) | copy-start | bytes 24580

commit v7 on v6

--- a/solution.py
+++ b/solution.py
@@ -13,7 +13,7 @@
 id_base = 32
 lanes = 128
 group = 16
-pieces = 3
+pieces = 2
 bf16 = jnp.bfloat16
 f32 = jnp.float32
 
@@ -195,7 +195,7 @@
             (((1,), (1,)), ((), ())),
             preferred_element_type=f32,
         ).T
-        total = total[:group] + total[group : 2 * group] + total[2 * group :]
+        total = sum(total[i * group : (i + 1) * group] for i in range(pieces))
         sums_ref[pl.ds(k, group, stride=count), :] = total
 
     got = [sums_ref[row * count : (row + 1) * count, :] for row in range(15)]

time: 23.1 us -> 23 us (level)
  no operation moved by 1% of the time
where the time goes in v7:
time: 23 us; the launch traced here: 22.6 us
  Pallas kernels  10.3 us (45%)
  starting transfers between devices  7.41 us (32%)
  waiting for transfers between devices  4.19 us (18%)
  between operations  0.66 us (3%)
    pallas_call x1, Pallas kernels, call_far(): pl.pallas_call(functools.partial(far_kernel, 'nb'), out_shape=(jax.ShapeD...  5.56 us
    all_to_all x1, starting transfers between devices, on_device(): lax.all_to_all(sums.reshape(hx_count, -1, sums.shape[1]), 'hx', split_axi...  5.18 us
    pallas_call x1, Pallas kernels, call_presum(): pl.pallas_call(functools.partial(presum_kernel, cap, uniq, tile), out_sha...  2.88 us
    all_to_all x1, waiting for transfers between devices, on_device(): lax.all_to_all(sums.reshape(hx_count, -1, sums.shape[1]), 'hx', split_axi...  2.47 us
    pallas_call x1, Pallas kernels, call_near(): pl.pallas_call(functools.partial(near_kernel, 'nb'), out_shape=(pltpu.VME...  1.9 us
    ppermute x1, waiting for transfers between devices, on_device(): lax.ppermute(sent, 'nb', even_pairs + [(j, i) for i, j in even_pairs])  1.72 us
    ppermute x1, starting transfers between devices, on_device(): lax.ppermute(sent, 'nb', even_pairs + [(j, i) for i, j in even_pairs])  1.58 us
    ppermute x1, starting transfers between devices, on_device(): odd = lax.ppermute(sent, 'nb', odd_pairs + [(j, i) for i, j in odd_pairs])  0.65 us
  transfers between devices with their start and end apart: 3, of which 2 were waited for; matrix products, arithmetic and copies ran while one was open for 0% of the time, Pallas kernels for 8%

profile of v7, /device:TPU:0, one launch (start us, length us, event | category | flops | bytes accessed | tf_op | source)
XLA Modules:
  0.0 22.6 jit_solution(15885438810121876859)
XLA Ops:
  0.6 2.9 %presum.1 = (bf16[128,1536]{1,0:T(8,128)(2,1)}, f32[6,16,128]{2,1,0:T(8,128)S(1)}, bf16[9,16,128]{2,1,0:T(8,128)(2,1)S(1)}, f32[16,128]{1,0:T(8,128)S(1)}, s32[1,8,16]{2,1,0:T(8,128)S(4)}) custom-call(s32[1,16]{1,0:T(1,128)} %counts_hbm.1, s32[1,512]{1,0:T(1,128)} %slots_hbm.1, bf16[1464,512]{1,0:T(8,128)(2,1)} %bitcast.12, f32[3,16,128]{2,1,0:T(8,128)} %bitcast.13, ...), custom_call_target="tpu_custom_call" | custom-call | tf_op jit(solution)/shard_map/presum/pallas_call | solution.py:395
  3.5 5.2 %all-to-all-start = ((bf16[8,16,1536]{2,1,0:T(8,128)(2,1)}), bf16[8,16,1536]{2,1,0:T(8,128)(2,1)S(1)}, u32[]{:S(2)}, u32[]{:S(2)}) async-start(bf16[8,16,1536]{2,1,0:T(8,128)(2,1)} %bitcast.4), calls=%async_computation | async-start | bytes 786432 | tf_op jit(solution)/shard_map/all_to_all | solution.py:453
  8.7 1.6 %collective-permute-start.1 = (bf16[9,16,128]{2,1,0:T(8,128)(2,1)S(1)}, bf16[9,16,128]{2,1,0:T(8,128)(2,1)S(1)}, u32[]{:S(2)}, u32[]{:S(2)}) collective-permute-start(bf16[9,16,128]{2,1,0:T(8,128)(2,1)S(1)} %get-tuple-element.13), channel_id=1, source_target_pairs={{0,1},{2,3},{1,0},{3,2},{4,5},{6,7},{5,4},{7,6},{8,9},{10,11},{9,8... | collective-permute-start | bytes 110600 | tf_op jit(solution)/shard_map/ppermute | solution.py:451
  10.3 0.7 %collective-permute-start = (bf16[9,16,128]{2,1,0:T(8,128)(2,1)S(1)}, bf16[9,16,128]{2,1,0:T(8,128)(2,1)S(1)}, u32[]{:S(2)}, u32[]{:S(2)}) collective-permute-start(bf16[9,16,128]{2,1,0:T(8,128)(2,1)S(1)} %get-tuple-element.13), channel_id=1, source_target_pairs={{1,2},{2,1},{5,6},{6,5},{9,10},{10,9},{13,14},{14,13},{17,18},{18,... | collective-permute-start | bytes 110600 | tf_op jit(solution)/shard_map/ppermute | solution.py:452
  10.9 1.7 %collective-permute-done.1.even_ref = bf16[9,16,128]{2,1,0:T(8,128)(2,1)S(1)} collective-permute-done((bf16[9,16,128]{2,1,0:T(8,128)(2,1)S(1)}, bf16[9,16,128]{2,1,0:T(8,128)(2,1)S(1)}, u32[]{:S(2)}, u32[]{:S(2)}) %collective-permute-start.1) | collective-permute-done | bytes 36896 | tf_op jit(solution)/shard_map/ppermute | solution.py:451
  12.7 0.0 collective-permute-done.odd_ref
  12.7 0.0 copy-start
  12.7 1.9 %near.1 = (f32[4,8,128]{2,1,0:T(8,128)S(1)}, bf16[2,1464,512]{2,1,0:T(8,128)(2,1)S(1)}) custom-call(s32[1,8,16]{2,1,0:T(8,128)S(4)} %get-tuple-element.11.neighbours_ref, f32[16,128]{1,0:T(8,128)S(1)} %get-tuple-element.15.live_ref, f32[6,16,128]{2,1,0:T(8,128)S(1)} %get-tuple-element.12.own_ref, bf16[9,16,128]{2,1,0:T(8,128)(2,1)S(1)} %collective-permute-done.odd_ref, ...), custom_call_target="tpu_custom_call" | custom-call | tf_op jit(solution)/shard_map/near/pallas_call | solution.py:339
  14.6 2.5 %all-to-all-done = bf16[8,16,1536]{2,1,0:T(8,128)(2,1)S(1)} async-done(((bf16[8,16,1536]{2,1,0:T(8,128)(2,1)}), bf16[8,16,1536]{2,1,0:T(8,128)(2,1)S(1)}, u32[]{:S(2)}, u32[]{:S(2)}) %all-to-all-start) | async-done | bytes 393248 | tf_op jit(solution)/shard_map/all_to_all | solution.py:453
  17.0 0.0 copy-done
  17.0 5.6 %far.1 = (bf16[1464,1024]{1,0:T(8,128)(2,1)}, f32[3,16,128]{2,1,0:T(8,128)}) custom-call(s32[1,8,16]{2,1,0:T(8,128)S(4)} %get-tuple-element.11.neighbours_ref, f32[6,16,128]{2,1,0:T(8,128)S(1)} %get-tuple-element.12.own_ref, bf16[9,16,128]{2,1,0:T(8,128)(2,1)S(1)} %collective-permute-done.odd_ref, bf16[9,16,128]{2,1,0:T(8,128)(2,1)S(1)} %collective-permute-done.1.even_ref, ...), custom_call_target="tpu_custom_call" | custom-call | tf_op jit(solution)/shard_map/far/pallas_call | solution.py:360
Async XLA Ops:
  3.5 13.5 %all-to-all-start = ((bf16[8,16,1536]{2,1,0:T(8,128)(2,1)}), bf16[8,16,1536]{2,1,0:T(8,128)(2,1)S(1)}, u32[]{:S(2)}, u32[]{:S(2)}) async-start(bf16[8,16,1536]{2,1,0:T(8,128)(2,1)} %bitcast.4), calls=%async_computation | async-start | bytes 786432 | tf_op jit(solution)/shard_map/all_to_all | solution.py:453
  8.7 4.0 %collective-permute-start.1 = (bf16[9,16,128]{2,1,0:T(8,128)(2,1)S(1)}, bf16[9,16,128]{2,1,0:T(8,128)(2,1)S(1)}, u32[]{:S(2)}, u32[]{:S(2)}) collective-permute-start(bf16[9,16,128]{2,1,0:T(8,128)(2,1)S(1)} %get-tuple-element.13), channel_id=1, source_target_pairs={{0,1},{2,3},{1,0},{3,2},{4,5},{6,7},{5,4},{7,6},{8,9},{10,11},{9,8... | collective-permute-start | bytes 110600 | tf_op jit(solution)/shard_map/ppermute | solution.py:451
  10.3 2.4 %collective-permute-start = (bf16[9,16,128]{2,1,0:T(8,128)(2,1)S(1)}, bf16[9,16,128]{2,1,0:T(8,128)(2,1)S(1)}, u32[]{:S(2)}, u32[]{:S(2)}) collective-permute-start(bf16[9,16,128]{2,1,0:T(8,128)(2,1)S(1)} %get-tuple-element.13), channel_id=1, source_target_pairs={{1,2},{2,1},{5,6},{6,5},{9,10},{10,9},{13,14},{14,13},{17,18},{18,... | collective-permute-start | bytes 110600 | tf_op jit(solution)/shard_map/ppermute | solution.py:452
  12.7 4.4 %copy-start = (s32[1,2,1024]{2,1,0:T(2,128)S(1)}, s32[1,2,1024]{2,1,0:T(2,128)}, u32[]{:S(2)}) copy-start(s32[1,2,1024]{2,1,0:T(2,128)} %picks_ref.1) | copy-start | bytes 24580
